TPU v7x, 1024 devices: a whole 4x8x16 slice. The times are simulated.
1024 devices in a mesh: dp: 16 (over y, core), expert: 64 (over x, z).
Axes of the slice: x: 4, y: 8, z: 16, core: 2. Of those that a mesh axis runs over, the one named last changes fastest.
Arguments:
- tokens: bfloat16 [16384, 2048], P(('dp', 'expert')), may hold values from -6 to 6
- expert_ids: int32 [16384, 8], P(('dp', 'expert')), may hold values from 0 to 63, all different within a row; in each aligned block of 16 rows (0 to 15, 16 to 31, ...) at most 4 rows name the same one
- route_weights: bfloat16 [16384, 8], P(('dp', 'expert')), may hold values from 0.049804688 to 0.5
- out_grad: bfloat16 [16384, 2048], P(('dp', 'expert')), may hold values from -6 to 6
- w_gate: bfloat16 [64, 2048, 384], P('expert'), may hold values from -0.125 to 0.125
- w_up: bfloat16 [64, 2048, 384], P('expert'), may hold values from -0.125 to 0.125
- w_down: bfloat16 [64, 384, 2048], P('expert'), may hold values from -0.3125 to 0.3125
Outputs:
- grad_tokens: bfloat16 [16384, 2048], P(('dp', 'expert'))
- grad_route: bfloat16 [16384, 8], P(('dp', 'expert'))
- grad_gate: float32 [64, 2048, 384], P('expert', 'dp')
- grad_up: float32 [64, 2048, 384], P('expert', 'dp')
- grad_down: float32 [64, 384, 2048], P('expert', None, 'dp')
Inputs may be any that keep to these rules, and one draw needn't show every extreme that they name: `expert_ids`: each token names 8 different experts. Among the 16 tokens of one device no expert is named more than 4 times, and in every draw some device names some expert exactly 4 times.
All inputs are finite; a program needn't handle non-finite values.
Results may differ from a plain program's by a relative error of at most 0.02.
Values may be sent and summed in bfloat16 or wider, within the bound.
No kernel may reach another device: no remote copies, remote signals or barrier semaphores. Data moves between devices by JAX's collectives and lax.ppermute only.
A program may use at most 32 MiB of HBM per device.

v0:
```python
import jax
import jax.numpy as jnp
from jax import lax
from jax.sharding import PartitionSpec as P


def expert_rows(inputs, cotangent, scaled, gate_w, up_w, down_w):
    pre_gate = jnp.dot(inputs, gate_w, preferred_element_type=jnp.float32)
    pre_up = jnp.dot(inputs, up_w, preferred_element_type=jnp.float32)
    sigma = jax.nn.sigmoid(pre_gate)
    hidden = (pre_gate * sigma * pre_up).astype(jnp.bfloat16)
    output = jnp.dot(hidden, down_w, preferred_element_type=jnp.float32)
    route_term = jnp.sum(output * cotangent.astype(jnp.float32), axis=1).astype(jnp.bfloat16)
    last_last = (((1,), (1,)), ((), ()))
    back_hidden = lax.dot_general(scaled, down_w, last_last, preferred_element_type=jnp.float32)
    gate_back = (back_hidden * pre_up * sigma * (1.0 + pre_gate * (1.0 - sigma))).astype(
        jnp.bfloat16
    )
    up_back = (back_hidden * pre_gate * sigma).astype(jnp.bfloat16)
    grad_in = lax.dot_general(gate_back, gate_w, last_last, preferred_element_type=jnp.float32)
    grad_in = (
        grad_in + lax.dot_general(up_back, up_w, last_last, preferred_element_type=jnp.float32)
    ).astype(jnp.bfloat16)
    return (hidden, gate_back, up_back, grad_in, route_term)


def shards(tokens, expert_ids, route_weights, out_grad, w_gate, w_up, w_down):
    tok_count, width = tokens.shape
    top = expert_ids.shape[1]
    experts = lax.axis_size("expert")
    groups = lax.axis_size("dp")
    cap = min(tok_count, max(2, 2 * tok_count * top // experts))
    slots = experts * cap
    first_first = (((0,), (0,)), ((), ()))
    flat_ids = expert_ids.reshape(-1)
    routed = flat_ids.shape[0]
    onehot = (flat_ids[:, None] == jnp.arange(experts, dtype=jnp.int32)[None, :]).astype(jnp.int32)
    running = jnp.cumsum(onehot, axis=0)
    position = jnp.sum(onehot * (running - 1), axis=1)
    slot_index = flat_ids * cap + position
    place = (slot_index[:, None] == jnp.arange(slots, dtype=jnp.int32)[None, :]).astype(
        jnp.bfloat16
    )
    owner = (
        (jnp.arange(routed, dtype=jnp.int32) // top)[:, None]
        == jnp.arange(tok_count, dtype=jnp.int32)[None, :]
    ).astype(jnp.bfloat16)
    dispatch = lax.dot_general(
        place, owner, first_first, preferred_element_type=jnp.float32
    ).astype(jnp.bfloat16)
    send_rows = (
        jnp.dot(dispatch, tokens, preferred_element_type=jnp.float32)
        .astype(jnp.bfloat16)
        .reshape(experts, cap, width)
    )
    send_weights = (
        lax.dot_general(
            place, route_weights.reshape(-1), first_first, preferred_element_type=jnp.float32
        )
        .astype(jnp.bfloat16)
        .reshape(experts, cap)
    )
    send_cot = (
        jnp.dot(dispatch, out_grad, preferred_element_type=jnp.float32)
        .astype(jnp.bfloat16)
        .reshape(experts, cap, width)
    )
    got_rows, got_weights = (
        lax.all_to_all(send_rows, "expert", split_axis=0, concat_axis=0, tiled=True),
        lax.all_to_all(send_weights, "expert", split_axis=0, concat_axis=0, tiled=True),
    )
    got_cot = lax.all_to_all(send_cot, "expert", split_axis=0, concat_axis=0, tiled=True)
    inputs = got_rows.reshape(slots, width)
    cotangent = got_cot.reshape(slots, width)
    scaled = (
        got_weights.reshape(slots, 1).astype(jnp.float32) * cotangent.astype(jnp.float32)
    ).astype(jnp.bfloat16)
    gate_w = w_gate[0]
    up_w = w_up[0]
    down_w = w_down[0]
    hidden, gate_back, up_back, grad_in, route_term = expert_rows(
        inputs, cotangent, scaled, gate_w, up_w, down_w
    )
    inverse = 1.0 / groups
    term_gate = lax.dot_general(inputs, gate_back, first_first, preferred_element_type=jnp.float32)
    term_up = lax.dot_general(inputs, up_back, first_first, preferred_element_type=jnp.float32)
    term_down = lax.dot_general(hidden, scaled, first_first, preferred_element_type=jnp.float32)
    sum_gate, sum_up, sum_down = (
        lax.psum_scatter(
            term_gate.astype(jnp.bfloat16), "dp", scatter_dimension=0, tiled=True
        ).astype(jnp.float32),
        lax.psum_scatter(
            term_up.astype(jnp.bfloat16), "dp", scatter_dimension=0, tiled=True
        ).astype(jnp.float32),
        lax.psum_scatter(
            term_down.astype(jnp.bfloat16), "dp", scatter_dimension=1, tiled=True
        ).astype(jnp.float32),
    )
    grad_gate = (sum_gate * inverse)[None]
    grad_up = (sum_up * inverse)[None]
    grad_down = (sum_down * inverse)[None]
    back_rows, back_route = (
        lax.all_to_all(
            grad_in.reshape(experts, cap, width), "expert", split_axis=0, concat_axis=0, tiled=True
        ),
        lax.all_to_all(
            route_term.reshape(experts, cap), "expert", split_axis=0, concat_axis=0, tiled=True
        ),
    )
    grad_tokens = lax.dot_general(
        dispatch, back_rows.reshape(slots, width), first_first, preferred_element_type=jnp.float32
    ).astype(jnp.bfloat16)
    grad_route = (
        jnp.dot(place, back_route.reshape(slots), preferred_element_type=jnp.float32)
        .astype(jnp.bfloat16)
        .reshape(tok_count, top)
    )
    return (grad_tokens, grad_route, grad_gate, grad_up, grad_down)


def solution(mesh):
    return jax.shard_map(
        shards,
        mesh=mesh,
        in_specs=(
            P(("dp", "expert"), None),
            P(("dp", "expert"), None),
            P(("dp", "expert"), None),
            P(("dp", "expert"), None),
            P("expert", None, None),
            P("expert", None, None),
            P("expert", None, None),
        ),
        out_specs=(
            P(("dp", "expert"), None),
            P(("dp", "expert"), None),
            P("expert", "dp", None),
            P("expert", "dp", None),
            P("expert", None, "dp"),
        ),
        check_vma=False,
    )
```

profile of v0, /device:TPU:1, one launch (start us, length us, event | category | flops | bytes accessed | tf_op | source)
XLA Modules:
  0.0 386.9 jit_solution(15824130878815213805)
XLA Ops:
  7.2 0.9 copy.19
  8.2 0.8 copy.18
  9.1 0.2 reduce_window_sum.11
  9.3 0.2 select_reduce_fusion
  9.5 0.2 fusion.16
  9.7 0.8 all_to_all.25
  10.4 22.8 %all-to-all-start = ((bf16[64,1,4]{2,1,0:T(2,128)(2,1)}), bf16[64,1,4]{2,1,0:T(2,128)(2,1)S(1)}, u32[]{:S(2)}, u32[]{:S(2)}) async-start(bf16[64,1,4]{2,1,0:T(2,128)(2,1)} %all_to_all.25), calls=%async_computation | async-start | bytes 65536 | tf_op jit(solution)/shard_map/all_to_all | solution.py:70
  33.2 0.2 convolution_convert_fusion.6
  33.5 1.3 convolution_convert_fusion.4
  34.8 1.2 reshape.104
  36.0 10.4 %all-to-all-done = bf16[64,1,4]{2,1,0:T(2,128)(2,1)S(1)} async-done(((bf16[64,1,4]{2,1,0:T(2,128)(2,1)}), bf16[64,1,4]{2,1,0:T(2,128)(2,1)S(1)}, u32[]{:S(2)}, u32[]{:S(2)}) %all-to-all-start) | async-done | bytes 544 | tf_op jit(solution)/shard_map/all_to_all | solution.py:70
  46.4 4.7 %all-to-all-start.1 = ((bf16[64,4,2048]{2,1,0:T(4,128)(2,1)}), bf16[64,4,2048]{2,1,0:T(4,128)(2,1)S(1)}, u32[]{:S(2)}, u32[]{:S(2)}) async-start(bf16[64,4,2048]{2,1,0:T(4,128)(2,1)} %reshape.104), calls=%async_computation.1 | async-start | bytes 2097152 | tf_op jit(solution)/shard_map/all_to_all | solution.py:72
  51.1 1.5 convolution_convert_fusion.3
  52.6 2.3 reshape.105
  54.8 44.9 %all-to-all-done.1 = bf16[64,4,2048]{2,1,0:T(4,128)(2,1)S(1)} async-done(((bf16[64,4,2048]{2,1,0:T(4,128)(2,1)}), bf16[64,4,2048]{2,1,0:T(4,128)(2,1)S(1)}, u32[]{:S(2)}, u32[]{:S(2)}) %all-to-all-start.1) | async-done | bytes 1048608 | tf_op jit(solution)/shard_map/all_to_all | solution.py:72
  99.8 12.0 %all-to-all-start.2 = ((bf16[64,4,2048]{2,1,0:T(4,128)(2,1)}), bf16[64,4,2048]{2,1,0:T(4,128)(2,1)}, u32[]{:S(2)}, u32[]{:S(2)}) async-start(bf16[64,4,2048]{2,1,0:T(4,128)(2,1)} %reshape.105), calls=%async_computation.2 | async-start | bytes 2097152 | tf_op jit(solution)/shard_map/all_to_all | solution.py:69
  112.0 1.5 multiply_convert_fusion.1
  113.5 2.1 convert_element_type.110
  115.6 46.2 %all-to-all-done.2 = bf16[64,4,2048]{2,1,0:T(4,128)(2,1)} async-done(((bf16[64,4,2048]{2,1,0:T(4,128)(2,1)}), bf16[64,4,2048]{2,1,0:T(4,128)(2,1)}, u32[]{:S(2)}, u32[]{:S(2)}) %all-to-all-start.2) | async-done | bytes 1048608 | tf_op jit(solution)/shard_map/all_to_all | solution.py:69
  161.8 1.3 reshape.106
  163.1 2.3 fusion.3
  165.4 0.7 fusion.9
  166.2 0.8 multiply_convert_fusion.3
  167.0 2.5 reshape.112
  169.5 3.4 convolution_convert_fusion
  172.9 2.6 copy.23
  175.5 1.9 convolution_convert_fusion.2
  177.5 2.9 fusion.11
  180.3 0.8 convert_element_type.134
  181.1 10.4 %all-to-all-start.4 = ((bf16[64,1,4]{2,1,0:T(2,128)(2,1)}), bf16[64,1,4]{2,1,0:T(2,128)(2,1)S(1)}, u32[]{:S(2)}, u32[]{:S(2)}) async-start(bf16[64,1,4]{2,1,0:T(2,128)(2,1)} %convert_element_type.134), calls=%async_computation.4 | async-start | bytes 65536 | tf_op jit(solution)/shard_map/all_to_all | solution.py:106
  191.5 2.2 fusion.1
  193.6 1.7 fusion
  195.4 2.2 reshape.107
  197.6 6.9 %all-to-all-done.4 = bf16[64,1,4]{2,1,0:T(2,128)(2,1)S(1)} async-done(((bf16[64,1,4]{2,1,0:T(2,128)(2,1)}), bf16[64,1,4]{2,1,0:T(2,128)(2,1)S(1)}, u32[]{:S(2)}, u32[]{:S(2)}) %all-to-all-start.4) | async-done | bytes 544 | tf_op jit(solution)/shard_map/all_to_all | solution.py:106
  204.5 7.8 %all-to-all-start.3 = ((bf16[64,4,2048]{2,1,0:T(4,128)(2,1)}), bf16[64,4,2048]{2,1,0:T(4,128)(2,1)}, u32[]{:S(2)}, u32[]{:S(2)}) async-start(bf16[64,4,2048]{2,1,0:T(4,128)(2,1)} %reshape.107), calls=%async_computation.3 | async-start | bytes 2097152 | tf_op jit(solution)/shard_map/all_to_all | solution.py:103
  212.3 1.9 convolution_convert_fusion.1
  214.4 0.1 reshape.116
  214.5 0.2 fusion.14
  214.8 0.7 copy.22
  215.5 23.1 %reduce-scatter.10.cloned.1.call-done = bf16[128,384]{1,0:T(8,128)(2,1)} async-done(((bf16[2048,384]{1,0:T(8,128)(2,1)}), bf16[128,384]{1,0:T(8,128)(2,1)}) %reduce-scatter.10.cloned.1.call-update) | async-done | bytes 98320
  238.6 1.0 copy.24
  239.6 0.7 multiply_bitcast_fusion
  240.3 67.8 %reduce-scatter.6.cloned.1.call-done = bf16[128,384]{1,0:T(8,128)(2,1)} async-done(((bf16[2048,384]{1,0:T(8,128)(2,1)}), bf16[128,384]{1,0:T(8,128)(2,1)}) %reduce-scatter.6.cloned.1.call-update) | async-done | bytes 98320 | tf_op jit(solution)/shard_map/reduce_scatter | solution.py:89
  308.1 1.6 multiply_bitcast_fusion.2
  309.7 66.8 %reduce-scatter.8.cloned.1.call-done = bf16[128,384]{1,0:T(8,128)(2,1)} async-done(((bf16[2048,384]{1,0:T(8,128)(2,1)}), bf16[128,384]{1,0:T(8,128)(2,1)}) %reduce-scatter.8.cloned.1.call-update) | async-done | bytes 98320 | tf_op jit(solution)/shard_map/reduce_scatter | solution.py:92
  376.5 1.6 multiply_bitcast_fusion.1
  378.1 1.3 reshape.108
  379.5 0.9 convolution_convert_fusion.5
  (27 shorter events, 0.9 us)
Async XLA Ops:
  7.2 159.0 %copy-start = (bf16[1,2048,384]{2,1,0:T(8,128)(2,1)S(1)}, bf16[1,2048,384]{2,1,0:T(8,128)(2,1)}, u32[]{:S(2)}) copy-start(bf16[1,2048,384]{2,1,0:T(8,128)(2,1)} %param.12) | copy-start | bytes 4718596
  10.4 36.0 %all-to-all-start = ((bf16[64,1,4]{2,1,0:T(2,128)(2,1)}), bf16[64,1,4]{2,1,0:T(2,128)(2,1)S(1)}, u32[]{:S(2)}, u32[]{:S(2)}) async-start(bf16[64,1,4]{2,1,0:T(2,128)(2,1)} %all_to_all.25), calls=%async_computation | async-start | bytes 65536 | tf_op jit(solution)/shard_map/all_to_all | solution.py:70
  36.0 15.1 %copy-start.4 = (bf16[16,2048]{1,0:T(8,128)(2,1)S(1)}, bf16[16,2048]{1,0:T(8,128)(2,1)}, u32[]{:S(2)}) copy-start(bf16[16,2048]{1,0:T(8,128)(2,1)} %param.7) | copy-start | bytes 196612
  46.4 53.3 %all-to-all-start.1 = ((bf16[64,4,2048]{2,1,0:T(4,128)(2,1)}), bf16[64,4,2048]{2,1,0:T(4,128)(2,1)S(1)}, u32[]{:S(2)}, u32[]{:S(2)}) async-start(bf16[64,4,2048]{2,1,0:T(4,128)(2,1)} %reshape.104), calls=%async_computation.1 | async-start | bytes 2097152 | tf_op jit(solution)/shard_map/all_to_all | solution.py:72
  99.8 13.7 %copy-start.1 = (bf16[64,4,2048]{2,1,0:T(4,128)(2,1)}, bf16[64,4,2048]{2,1,0:T(4,128)(2,1)S(1)}, u32[]{:S(2)}) copy-start(bf16[64,4,2048]{2,1,0:T(4,128)(2,1)S(1)} %all-to-all-done.1) | copy-start | bytes 3145732
  99.8 62.0 %all-to-all-start.2 = ((bf16[64,4,2048]{2,1,0:T(4,128)(2,1)}), bf16[64,4,2048]{2,1,0:T(4,128)(2,1)}, u32[]{:S(2)}, u32[]{:S(2)}) async-start(bf16[64,4,2048]{2,1,0:T(4,128)(2,1)} %reshape.105), calls=%async_computation.2 | async-start | bytes 2097152 | tf_op jit(solution)/shard_map/all_to_all | solution.py:69
  111.7 126.9 %reduce-scatter.10.cloned.1.call-start = ((), (), s32[]{:S(2)}) async-start(), calls=%async_computation.10 | async-start | bytes 1671168
  163.1 2.3 copy-start.2
  163.1 2.3 copy-start.3
  175.5 132.7 %reduce-scatter.6.cloned.1.call-start = ((), (), s32[]{:S(2)}) async-start(), calls=%async_computation.8 | async-start | bytes 1671168 | tf_op jit(solution)/shard_map/reduce_scatter | solution.py:89
  181.1 23.4 %all-to-all-start.4 = ((bf16[64,1,4]{2,1,0:T(2,128)(2,1)}), bf16[64,1,4]{2,1,0:T(2,128)(2,1)S(1)}, u32[]{:S(2)}, u32[]{:S(2)}) async-start(bf16[64,1,4]{2,1,0:T(2,128)(2,1)} %convert_element_type.134), calls=%async_computation.4 | async-start | bytes 65536 | tf_op jit(solution)/shard_map/all_to_all | solution.py:106
  204.5 173.6 %all-to-all-start.3 = ((bf16[64,4,2048]{2,1,0:T(4,128)(2,1)}), bf16[64,4,2048]{2,1,0:T(4,128)(2,1)}, u32[]{:S(2)}, u32[]{:S(2)}) async-start(bf16[64,4,2048]{2,1,0:T(4,128)(2,1)} %reshape.107), calls=%async_computation.3 | async-start | bytes 2097152 | tf_op jit(solution)/shard_map/all_to_all | solution.py:103
  212.3 164.3 %reduce-scatter.8.cloned.1.call-start = ((), (), s32[]{:S(2)}) async-start(), calls=%async_computation.9 | async-start | bytes 1671168 | tf_op jit(solution)/shard_map/reduce_scatter | solution.py:92
Sparse Core Ops, SparseCore 0:
  175.6 62.9 reduce-scatter.9
  242.4 65.7 reduce-scatter.5
  311.6 64.9 reduce-scatter.7
where the time goes:
time: 388 us; the launch traced here: 387 us
  waiting for transfers between devices  266 us (69%)
  starting transfers between devices  57.7 us (15%)
  matrix products  22.1 us (6%)
  local copies, waits for them, and re-layouts  20.9 us (5%)
  between operations  14 us (4%)
  other arithmetic  5.99 us (2%)
    reduce_scatter x1, waiting for transfers between devices, shards(): lax.psum_scatter(term_gate.astype(jnp.bfloat16), 'dp', scatter_dimension=...  67.8 us
    reduce_scatter x1, waiting for transfers between devices, shards(): lax.psum_scatter(term_up.astype(jnp.bfloat16), 'dp', scatter_dimension=0,...  66.8 us
    all_to_all x1, waiting for transfers between devices, shards(): lax.all_to_all(send_rows, 'expert', split_axis=0, concat_axis=0, tiled=True)  46.2 us
    all_to_all x1, waiting for transfers between devices, shards(): lax.all_to_all(send_cot, 'expert', split_axis=0, concat_axis=0, tiled=True)  44.9 us
    unnamed x4, waiting for transfers between devices  23.2 us
    all_to_all x1, starting transfers between devices, shards(): lax.all_to_all(send_weights, 'expert', split_axis=0, concat_axis=0, tiled...  22.8 us
    all_to_all x1, starting transfers between devices, shards(): lax.all_to_all(send_rows, 'expert', split_axis=0, concat_axis=0, tiled=True)  12 us
    all_to_all x1, waiting for transfers between devices, shards(): lax.all_to_all(send_weights, 'expert', split_axis=0, concat_axis=0, tiled...  10.4 us
  transfers between devices with their start and end apart: 8, of which 7 were waited for; matrix products, arithmetic and copies ran while one was open for 8% of the time, Pallas kernels for 0%

commit v1 on v0

v1 whole, which is shorter than its diff:
```python
import jax
import jax.numpy as jnp
from jax import lax
from jax.sharding import Mesh
from jax.sharding import PartitionSpec as P

BF = jnp.bfloat16
F32 = jnp.float32
META = 128
FIRST = (((0,), (0,)), ((), ()))
LAST = (((1,), (1,)), ((), ()))


def shards(tokens, expert_ids, route_weights, out_grad, w_gate, w_up, w_down):
    tok, width = tokens.shape
    top = expert_ids.shape[1]
    nx, nh, nl = lax.axis_size("x"), lax.axis_size("zh"), lax.axis_size("zl")
    ny, nc = lax.axis_size("y"), lax.axis_size("core")
    experts = nx * nh * nl
    cap = min(tok, max(2, 2 * tok * top // experts))
    held = nh * tok
    dests = nx * nl
    per = nh * cap
    slots = dests * per

    meta = jnp.concatenate(
        [
            expert_ids.astype(BF),
            route_weights,
            jnp.zeros((tok, META - 2 * top), BF),
        ],
        axis=1,
    )
    packed = jnp.concatenate([tokens, out_grad, meta], axis=1)
    gathered = lax.all_gather(packed, "zh", axis=0, tiled=True)
    rows = gathered[:, :width]
    cots = gathered[:, width : 2 * width]
    ids = gathered[:, 2 * width : 2 * width + top].astype(jnp.int32)
    weights = gathered[:, 2 * width + top : 2 * width + 2 * top].astype(F32)

    dest = jnp.arange(dests, dtype=jnp.int32)
    dest_ids = (dest // nl) * (nh * nl) + lax.axis_index("zh") * nl + dest % nl
    named = ids[None, :, :] == dest_ids[:, None, None]
    match = jnp.any(named, axis=2)
    weight_of = jnp.sum(jnp.where(named, weights[None], 0.0), axis=2)
    t = jnp.arange(held, dtype=jnp.int32)
    earlier = ((t[:, None] < t[None, :]) & (t[:, None] // tok == t[None, :] // tok)).astype(BF)
    position = jnp.dot(match.astype(BF), earlier, preferred_element_type=F32).astype(jnp.int32)
    place = (t // tok) * cap + position
    select = (
        match[:, None, :] & (place[:, None, :] == jnp.arange(per, dtype=jnp.int32)[None, :, None])
    )
    pick = select.astype(BF).reshape(slots, held)
    scaled_pick = jnp.where(select, weight_of[:, None, :], 0.0).astype(BF).reshape(slots, held)
    send_rows = jnp.dot(pick, rows, preferred_element_type=F32).astype(BF)
    send_cots = jnp.dot(scaled_pick, cots, preferred_element_type=F32).astype(BF)

    def forward(a):
        return lax.all_to_all(
            a.reshape(dests, per, -1), ("x", "zl"), split_axis=0, concat_axis=0, tiled=True
        ).reshape(slots, -1)

    inputs = forward(send_rows)
    scaled = forward(send_cots)

    gate_w, up_w, down_w = w_gate[0], w_up[0], w_down[0]
    pre_gate = jnp.dot(inputs, gate_w, preferred_element_type=F32)
    pre_up = jnp.dot(inputs, up_w, preferred_element_type=F32)
    sigma = jax.nn.sigmoid(pre_gate)
    hidden = (pre_gate * sigma * pre_up).astype(BF)
    back_hidden = lax.dot_general(scaled, down_w, LAST, preferred_element_type=F32)
    weighted_route = jnp.sum(hidden.astype(F32) * back_hidden, axis=1, keepdims=True)
    gate_back = (back_hidden * pre_up * sigma * (1.0 + pre_gate * (1.0 - sigma))).astype(BF)
    up_back = (back_hidden * pre_gate * sigma).astype(BF)

    part = jnp.stack(
        [
            lax.dot_general(inputs, gate_back, FIRST, preferred_element_type=F32).astype(BF),
            lax.dot_general(inputs, up_back, FIRST, preferred_element_type=F32).astype(BF),
            lax.dot_general(scaled, hidden, FIRST, preferred_element_type=F32).astype(BF),
        ]
    )
    block = width // (ny * nc)
    ff = part.shape[2]
    part = part.reshape(3, ny, nc, block, ff)
    core = lax.axis_index("core")
    other = lax.dynamic_index_in_dim(part, 1 - core, 2, keepdims=False)
    own = lax.dynamic_index_in_dim(part, core, 2, keepdims=False)
    came = lax.ppermute(other, "core", [(0, 1), (1, 0)])
    pair = (own.astype(F32) + came.astype(F32)).astype(BF)
    pair = pair.transpose(1, 0, 2, 3).reshape(ny * 3 * block, ff)
    total = lax.psum_scatter(pair, "y", scatter_dimension=0, tiled=True)
    total = total.reshape(3, block, ff).astype(F32) * (1.0 / (ny * nc))

    grad_in = lax.dot_general(gate_back, gate_w, LAST, preferred_element_type=F32)
    grad_in = (
        grad_in + lax.dot_general(up_back, up_w, LAST, preferred_element_type=F32)
    ).astype(BF)
    high = weighted_route.astype(BF)
    low = (weighted_route - high.astype(F32)).astype(BF)
    back = jnp.concatenate([grad_in, high, low, jnp.zeros((slots, META - 2), BF)], axis=1)
    back = forward(back)
    token_part = lax.dot_general(
        pick, back[:, :width], FIRST, preferred_element_type=F32
    ).astype(BF)
    route_rows = back[:, width].astype(F32) + back[:, width + 1].astype(F32)
    by_dest = jnp.sum(
        jnp.where(select, route_rows.reshape(dests, per)[:, :, None], 0.0), axis=1
    )
    route_part = jnp.sum(jnp.where(named, by_dest[:, :, None], 0.0), axis=0) / weights
    outgoing = jnp.concatenate(
        [token_part, route_part.astype(BF), jnp.zeros((held, META - top), BF)], axis=1
    )
    parts = lax.all_to_all(
        outgoing.reshape(nh, tok, -1), "zh", split_axis=0, concat_axis=0, tiled=True
    )
    summed = jnp.sum(parts.astype(F32), axis=0)
    grad_tokens = summed[:, :width].astype(BF)
    grad_route = summed[:, width : width + top].astype(BF)
    return (grad_tokens, grad_route, total[0][None], total[1][None], total[2].T[None])


def solution(mesh):
    groups, experts = mesh.devices.shape
    n = round(experts ** (1 / 3))
    fine = Mesh(
        mesh.devices.reshape(groups // 2, 2, n, n, n), ("y", "core", "x", "zh", "zl")
    )
    dp = ("y", "core")
    ex = ("x", "zh", "zl")
    rows = P(dp + ex, None)
    return jax.shard_map(
        shards,
        mesh=fine,
        in_specs=(rows, rows, rows, rows) + (P(ex, None, None),) * 3,
        out_specs=(rows, rows, P(ex, dp, None), P(ex, dp, None), P(ex, None, dp)),
        check_vma=False,
    )
```

time: 388 us -> 206 us (0.53)
  waiting for transfers between devices: 266 us -> 73.3 us
  blocking collectives: 0 us -> 57.6 us
  starting transfers between devices: 57.7 us -> 26.1 us
  local copies, waits for them, and re-layouts: 20.9 us -> 12 us
  matrix products: 22.1 us -> 14.6 us
    reduce_scatter x2 -> x1, waiting for transfers between devices: 135 us -> 0.01 us  [shards(): total = lax.psum_scatter(pair, 'y', scatter_dimension=0, tiled=True)]
    all_to_all x5 -> x3, waiting for transfers between devices: 108 us -> 73.2 us  [forward(): lax.all_to_all(a.reshape(dests, per, -1), ('x', 'zl'), split_axis=0, conc...]
    all_to_all x5 -> x3, starting transfers between devices: 57.5 us -> 22.4 us  [forward(): lax.all_to_all(a.reshape(dests, per, -1), ('x', 'zl'), split_axis=0, conc...]
    all_gather x0 -> x1, blocking collectives: none -> 33.3 us  [shards(): gathered = lax.all_gather(packed, 'zh', axis=0, tiled=True)]
    all_to_all x0 -> x1, blocking collectives: none -> 24.3 us  [shards(): lax.all_to_all(outgoing.reshape(nh, tok, -1), 'zh', split_axis=0, concat_...]
    unnamed x4 -> x1, waiting for transfers between devices: 23.2 us -> 0.02 us
    reshape x9 -> x0, local copies, waits for them, and re-layouts: 8.78 us -> none  [the longest x1 2.26 us: shards(): send_rows = jnp.dot(dispatch, tokens, preferred_element_type=jnp.float32)...]
    dot_general x15 -> x12, matrix products: 22.1 us -> 14.6 us  [the longest x1 2.69 us: shards(): lax.dot_general(scaled, down_w, LAST, preferred_element_type=F32)]
  transfers between devices with their start and end apart: 8 -> 5, of which waited for: 7 -> 3; matrix products, arithmetic and copies ran while one was open for 8% -> 8% of each run, Pallas kernels for 0% -> 0%
where the time goes in v1:
time: 206 us
  waiting for transfers between devices  73.3 us (36%)
  blocking collectives  57.6 us (28%)
  starting transfers between devices  26.1 us (13%)
  matrix products  14.6 us (7%)
  between operations  14.2 us (7%)
  local copies, waits for them, and re-layouts  12 us (6%)
  other arithmetic  8.05 us (4%)
    all_to_all x3, waiting for transfers between devices, forward(): lax.all_to_all(a.reshape(dests, per, -1), ('x', 'zl'), split_axis=0, conc...  73.2 us
    all_gather x1, blocking collectives, shards(): gathered = lax.all_gather(packed, 'zh', axis=0, tiled=True)  33.3 us
    all_to_all x1, blocking collectives, shards(): lax.all_to_all(outgoing.reshape(nh, tok, -1), 'zh', split_axis=0, concat_...  24.3 us
    all_to_all x3, starting transfers between devices, forward(): lax.all_to_all(a.reshape(dests, per, -1), ('x', 'zl'), split_axis=0, conc...  22.4 us
    unnamed x10, local copies, waits for them, and re-layouts  4.79 us
    convert_element_type x1, other arithmetic, shards(): pair = (own.astype(F32) + came.astype(F32)).astype(BF)  4.67 us
  transfers between devices with their start and end apart: 5, of which 3 were waited for; matrix products, arithmetic and copies ran while one was open for 8% of the time, Pallas kernels for 0%

profile of v1, /device:TPU:1, one launch (start us, length us, event | category | flops | bytes accessed | tf_op | source)
XLA Modules:
  0.0 205.8 jit_solution(7857271012894193558)
XLA Ops:
  7.2 0.1 eq.62
  7.3 0.8 convert_element_type.133
  8.1 0.1 copy.66
  8.2 0.8 copy.67
  8.9 1.0 concatenate.13
  9.9 33.3 %all_gather.3 = bf16[64,4224]{1,0:T(8,128)(2,1)S(1)} all-gather(bf16[16,4224]{1,0:T(8,128)(2,1)S(1)} %concatenate.13), channel_id=1, replica_groups=mesh['y'=8,'core'=2,'x'=4,'zh'=4,'zl'=4] {'zh'}, dimensions={0}, use_global_device_ids=true | all-gather | bytes 675840 | tf_op jit(solution)/shard_map/all_gather | solution.py:35
  43.3 0.1 compare_reduce_fusion
  43.5 0.2 fusion.11
  43.7 0.1 fusion.17
  43.8 1.4 convolution_convert_fusion.3
  45.2 14.2 %all-to-all-start.1 = ((bf16[16,16,2048]{2,1,0:T(8,128)(2,1)}), bf16[16,16,2048]{2,1,0:T(8,128)(2,1)S(1)}, u32[]{:S(2)}, u32[]{:S(2)}) async-start(bf16[16,16,2048]{2,1,0:T(8,128)(2,1)} %bitcast.85), calls=%async_computation.1 | async-start | bytes 2097152 | tf_op jit(solution)/shard_map/all_to_all | solution.py:59
  59.5 0.1 fusion.18
  59.6 0.1 fusion.15
  59.7 1.4 convolution_convert_fusion.4
  61.1 25.2 %all-to-all-done.1 = bf16[16,16,2048]{2,1,0:T(8,128)(2,1)S(1)} async-done(((bf16[16,16,2048]{2,1,0:T(8,128)(2,1)}), bf16[16,16,2048]{2,1,0:T(8,128)(2,1)S(1)}, u32[]{:S(2)}, u32[]{:S(2)}) %all-to-all-start.1) | async-done | bytes 1048608 | tf_op jit(solution)/shard_map/all_to_all | solution.py:59
  86.4 4.5 %all-to-all-start = ((bf16[16,16,2048]{2,1,0:T(8,128)(2,1)}), bf16[16,16,2048]{2,1,0:T(8,128)(2,1)}, u32[]{:S(2)}, u32[]{:S(2)}) async-start(bf16[16,16,2048]{2,1,0:T(8,128)(2,1)} %bitcast.84), calls=%async_computation | async-start | bytes 2097152 | tf_op jit(solution)/shard_map/all_to_all | solution.py:59
  90.9 2.1 %fusion.7 = f32[256,384]{1,0:T(8,128)S(1)} fusion(bf16[256,2048]{1,0:T(8,128)(2,1)S(1)} %bitcast.73, bf16[1,2048,384]{2,1,0:T(8,128)(2,1)} %param.12), kind=kOutput, calls=%fused_computation.18 | convolution fusion | flops 402653184 | bytes 3014656 | tf_op jit(solution)/shard_map/dot_general | solution.py:68
  93.0 1.5 fusion.4
  94.5 23.4 %all-to-all-done = bf16[16,16,2048]{2,1,0:T(8,128)(2,1)} async-done(((bf16[16,16,2048]{2,1,0:T(8,128)(2,1)}), bf16[16,16,2048]{2,1,0:T(8,128)(2,1)}, u32[]{:S(2)}, u32[]{:S(2)}) %all-to-all-start) | async-done | bytes 1048608 | tf_op jit(solution)/shard_map/all_to_all | solution.py:59
  117.9 2.7 %multiply_reduce_fusion = (f32[256]{0:T(256)S(1)}, bf16[256,384]{1,0:T(8,128)(2,1)S(1)}, bf16[256,384]{1,0:T(8,128)(2,1)S(1)}, bf16[256,384]{1,0:T(8,128)(2,1)S(1)}) fusion(f32[256,384]{1,0:T(8,128)S(1)} %fusion.7, f32[256,384]{1,0:T(8,128)} %fusion.4, bf16[256,2048]{1,0:T(8,128)(2,1)} %bitcast.4, bf16[1,384,2048]{2,1,0:T(8,128)(2,1)} %param.13), kind=kOutput, calls=%fused_computation.26 | convolution fusion | flops 404520704 | bytes 3998720 | tf_op jit(solution)/shard_map/dot_general | solution.py:71
  120.6 2.0 convolution_convert_fusion
  122.6 0.7 convolution_convert_fusion.1
  123.3 0.7 convolution_convert_fusion.2
  124.1 0.7 pad_maximum_fusion
  124.7 1.9 constant_dynamic-slice_fusion.1
  126.7 1.7 copy.87
  128.4 3.7 %collective-permute-start = (bf16[3,8,128,384]{3,2,0,1:T(8,128)(2,1)}, bf16[3,8,128,384]{3,2,0,1:T(8,128)(2,1)}, u32[]{:S(2)}, u32[]{:S(2)}) collective-permute-start(bf16[3,8,128,384]{3,2,0,1:T(8,128)(2,1)} %bitcast.72), channel_id=1, source_target_pairs={{0,64},{64,0},{1,65},{65,1},{2,66},{66,2},{3,67},{67,3},{4,68},{68... | collective-permute-start | bytes 7077896 | tf_op jit(solution)/shard_map/ppermute | solution.py:89
  132.1 0.2 copy.70
  132.3 0.2 copy.71
  132.5 0.7 fusion.2
  133.3 0.7 copy-done.1
  133.9 0.8 fusion.1
  134.7 1.9 concatenate.15
  136.7 3.7 %all-to-all-start.2 = ((bf16[16,16,2176]{2,1,0:T(8,128)(2,1)}), bf16[16,16,2176]{2,1,0:T(8,128)(2,1)S(1)}, u32[]{:S(2)}, u32[]{:S(2)}) async-start(bf16[16,16,2176]{2,1,0:T(8,128)(2,1)} %concatenate.15), calls=%async_computation.2 | async-start | bytes 2228224 | tf_op jit(solution)/shard_map/all_to_all | solution.py:59
  140.4 4.7 %fusion = bf16[3,8,128,384]{3,2,0,1:T(8,128)(2,1)} fusion(bf16[3,8,128,384]{3,2,0,1:T(8,128)(2,1)} %collective-permute-done, bf16[3,8,1,128,384]{4,3,2,1,0:T(8,128)(2,1)} %get-tuple-element.44), kind=kLoop, calls=%fused_computation.2 | loop fusion | flops 4718592 | bytes 7077888 | tf_op jit(solution)/shard_map/convert_element_type | solution.py:90
  145.1 24.6 %all-to-all-done.2 = bf16[16,16,2176]{2,1,0:T(8,128)(2,1)S(1)} async-done(((bf16[16,16,2176]{2,1,0:T(8,128)(2,1)}), bf16[16,16,2176]{2,1,0:T(8,128)(2,1)S(1)}, u32[]{:S(2)}, u32[]{:S(2)}) %all-to-all-start.2) | async-done | bytes 1114144 | tf_op jit(solution)/shard_map/all_to_all | solution.py:59
  169.7 0.2 add_reduce_fusion
  169.9 0.1 select_reduce_fusion
  170.1 0.1 fusion.19
  170.2 0.1 copy.72
  170.3 0.3 convolution_convert_fusion.5
  170.6 0.1 concatenate.16
  170.7 24.3 %all_to_all.20 = bf16[4,16,2176]{2,1,0:T(8,128)(2,1)S(1)} all-to-all(bf16[4,16,2176]{2,1,0:T(8,128)(2,1)S(1)} %bitcast.86), channel_id=1, replica_groups=mesh['y'=8,'core'=2,'x'=4,'zh'=4,'zl'=4] {'zh'}, dimensions={0} | all-to-all | bytes 557056 | tf_op jit(solution)/shard_map/all_to_all | solution.py:114
  195.0 0.6 slice.66
  195.7 0.7 copy.76
  196.3 1.0 convert_multiply_fusion
  197.3 0.8 slice_bitcast_fusion
  198.1 0.8 copy.77
  (24 shorter events, 0.6 us)
Async XLA Ops:
  7.2 85.8 %copy-start = (bf16[1,2048,384]{2,1,0:T(8,128)(2,1)S(1)}, bf16[1,2048,384]{2,1,0:T(8,128)(2,1)}, u32[]{:S(2)}) copy-start(bf16[1,2048,384]{2,1,0:T(8,128)(2,1)} %param.11) | copy-start | bytes 4718596
  45.2 41.2 %all-to-all-start.1 = ((bf16[16,16,2048]{2,1,0:T(8,128)(2,1)}), bf16[16,16,2048]{2,1,0:T(8,128)(2,1)S(1)}, u32[]{:S(2)}, u32[]{:S(2)}) async-start(bf16[16,16,2048]{2,1,0:T(8,128)(2,1)} %bitcast.85), calls=%async_computation.1 | async-start | bytes 2097152 | tf_op jit(solution)/shard_map/all_to_all | solution.py:59
  86.4 31.5 %all-to-all-start = ((bf16[16,16,2048]{2,1,0:T(8,128)(2,1)}), bf16[16,16,2048]{2,1,0:T(8,128)(2,1)}, u32[]{:S(2)}, u32[]{:S(2)}) async-start(bf16[16,16,2048]{2,1,0:T(8,128)(2,1)} %bitcast.84), calls=%async_computation | async-start | bytes 2097152 | tf_op jit(solution)/shard_map/all_to_all | solution.py:59
  128.4 12.0 %collective-permute-start = (bf16[3,8,128,384]{3,2,0,1:T(8,128)(2,1)}, bf16[3,8,128,384]{3,2,0,1:T(8,128)(2,1)}, u32[]{:S(2)}, u32[]{:S(2)}) collective-permute-start(bf16[3,8,128,384]{3,2,0,1:T(8,128)(2,1)} %bitcast.72), channel_id=1, source_target_pairs={{0,64},{64,0},{1,65},{65,1},{2,66},{66,2},{3,67},{67,3},{4,68},{68... | collective-permute-start | bytes 7077896 | tf_op jit(solution)/shard_map/ppermute | solution.py:89
  132.5 1.4 copy-start.1
  136.7 33.0 %all-to-all-start.2 = ((bf16[16,16,2176]{2,1,0:T(8,128)(2,1)}), bf16[16,16,2176]{2,1,0:T(8,128)(2,1)S(1)}, u32[]{:S(2)}, u32[]{:S(2)}) async-start(bf16[16,16,2176]{2,1,0:T(8,128)(2,1)} %concatenate.15), calls=%async_computation.2 | async-start | bytes 2228224 | tf_op jit(solution)/shard_map/all_to_all | solution.py:59
  140.4 56.0 %reduce-scatter.2.cloned.1.call-start = ((), (), s32[]{:S(2)}) async-start(), calls=%async_computation.5 | async-start | bytes 2654208 | tf_op jit(solution)/shard_map/reduce_scatter | solution.py:92
Sparse Core Ops, SparseCore 0:
  145.2 44.2 reduce-scatter.1

commit v2 on v1

v2 whole, which is shorter than its diff:
```python
import functools

import jax
import jax.numpy as jnp
from jax import lax
from jax.experimental import pallas as pl
from jax.experimental.pallas import tpu as pltpu
from jax.sharding import Mesh
from jax.sharding import PartitionSpec as P

BF = jnp.bfloat16
F32 = jnp.float32
META = 128
VMEM = pl.BlockSpec(memory_space=pltpu.VMEM)
FIRST = (((0,), (0,)), ((), ()))
LAST = (((1,), (1,)), ((), ()))


def call(body, outs, flops, moved):
    return pl.pallas_call(
        body,
        out_shape=outs,
        compiler_params=pltpu.CompilerParams(vmem_limit_bytes=30 * 1024 * 1024),
        cost_estimate=pl.CostEstimate(flops=flops, bytes_accessed=moved, transcendentals=0),
    )


def select_body(tok, cap, top, held_ref, dest_ref, send_ref, pick_ref):
    held = held_ref.shape[0]
    slots, width = send_ref.shape[0], send_ref.shape[1] // 2
    meta = held_ref[:, 2 * width :].astype(F32)
    dest = dest_ref[...]
    match = jnp.zeros((held, slots), F32)
    weight = jnp.zeros((held, slots), F32)
    for k in range(top):
        same = meta[:, k : k + 1] == dest
        match = jnp.where(same, 1.0, match)
        weight = jnp.where(same, meta[:, top + k : top + k + 1], weight)
    row = lax.broadcasted_iota(jnp.int32, (held, held), 0)
    col = lax.broadcasted_iota(jnp.int32, (held, held), 1)
    earlier = jnp.where((col < row) & (col // tok == row // tok), 1.0, 0.0).astype(BF)
    position = jnp.dot(earlier, match.astype(BF), preferred_element_type=F32).astype(jnp.int32)
    token = lax.broadcasted_iota(jnp.int32, (held, slots), 0)
    slot = lax.broadcasted_iota(jnp.int32, (held, slots), 1) % (held // tok * cap)
    pick = (match > 0.5) & (position + token // tok * cap == slot) & (position < cap)
    flat = jnp.where(pick, 1.0, 0.0).astype(BF)
    scaled = jnp.where(pick, weight, 0.0).astype(BF)
    pick_ref[...] = flat
    for half, chosen in ((0, flat), (1, scaled)):
        send_ref[:, half * width : (half + 1) * width] = lax.dot_general(
            chosen,
            held_ref[:, half * width : (half + 1) * width],
            FIRST,
            preferred_element_type=F32,
        ).astype(BF)


def expert_body(nblock, core_ref, came_ref, gate_ref, up_ref, down_ref, hidden_ref, gate_back_ref, up_back_ref, route_ref, other_ref):
    width = came_ref.shape[1] // 2
    inputs, scaled = came_ref[:, :width], came_ref[:, width:]
    pre_gate = jnp.dot(inputs, gate_ref[...], preferred_element_type=F32)
    pre_up = jnp.dot(inputs, up_ref[...], preferred_element_type=F32)
    back_hidden = lax.dot_general(scaled, down_ref[...], LAST, preferred_element_type=F32)
    sigma = 1.0 / (1.0 + jnp.exp(-pre_gate))
    active = pre_gate * sigma
    hidden = (active * pre_up).astype(BF)
    gate_back = (back_hidden * pre_up * sigma * (1.0 + pre_gate * (1.0 - sigma))).astype(BF)
    up_back = (back_hidden * active).astype(BF)
    hidden_ref[...] = hidden
    gate_back_ref[...] = gate_back
    up_back_ref[...] = up_back
    route = jnp.sum(hidden.astype(F32) * back_hidden, axis=1, keepdims=True)
    high = route.astype(BF).astype(F32)
    lane = lax.broadcasted_iota(jnp.int32, route_ref.shape, 1)
    route_ref[...] = jnp.where(
        lane == 0, high, jnp.where(lane == 1, route - high, 0.0)
    ).astype(BF)
    weight_terms(nblock, 1 - core_ref[0], came_ref, hidden, gate_back, up_back, None, other_ref)


def weight_terms(nblock, core, came_ref, hidden, gate_back, up_back, add_ref, out_ref):
    width = came_ref.shape[1] // 2
    block = width // nblock
    for y in range(nblock // 2):
        for which, (base, right) in enumerate(
            ((0, gate_back), (0, up_back), (width, hidden))
        ):
            at = pl.multiple_of(base + (2 * y + core) * block, block)
            term = lax.dot_general(
                came_ref[:, pl.ds(at, block)], right, FIRST, preferred_element_type=F32
            )
            if add_ref is not None:
                term = term + add_ref[y, which].astype(F32)
            out_ref[y, which] = term.astype(BF)


def own_body(nblock, core_ref, came_ref, hidden_ref, gate_back_ref, up_back_ref, add_ref, out_ref):
    weight_terms(
        nblock, core_ref[0], came_ref, hidden_ref[...], gate_back_ref[...], up_back_ref[...], add_ref, out_ref
    )


def back_body(gate_back_ref, up_back_ref, route_ref, gate_ref, up_ref, out_ref):
    width = gate_ref.shape[0]
    out = lax.dot_general(gate_back_ref[...], gate_ref[...], LAST, preferred_element_type=F32)
    out = out + lax.dot_general(up_back_ref[...], up_ref[...], LAST, preferred_element_type=F32)
    out_ref[:, :width] = out.astype(BF)
    out_ref[:, width:] = route_ref[...]


def combine_body(top, back_ref, pick_ref, meta_ref, dest_ref, out_ref):
    width = back_ref.shape[1] - META
    pick = pick_ref[...]
    out_ref[:, :width] = jnp.dot(pick, back_ref[:, :width], preferred_element_type=F32).astype(BF)
    lane8 = lax.broadcasted_iota(jnp.int32, (8, META), 1)
    pair = jnp.where(lane8 < 2, 1.0, 0.0).astype(BF)
    route = lax.dot_general(pair, back_ref[:, width:], LAST, preferred_element_type=F32)[0:1]
    mine = jnp.where(pick.astype(F32) > 0.5, route, 0.0)
    meta = meta_ref[...].astype(F32)
    dest = dest_ref[...]
    lane = lax.broadcasted_iota(jnp.int32, (pick.shape[0], META), 1)
    routes = jnp.zeros((pick.shape[0], META), F32)
    for k in range(top):
        value = jnp.sum(
            jnp.where(meta[:, k : k + 1] == dest, mine, 0.0), axis=1, keepdims=True
        )
        routes = jnp.where(lane == k, value / meta[:, top + k : top + k + 1], routes)
    out_ref[:, width:] = routes.astype(BF)


def shards(tokens, expert_ids, route_weights, out_grad, w_gate, w_up, w_down):
    tok, width = tokens.shape
    top = expert_ids.shape[1]
    ff = w_gate.shape[2]
    nx, nh, nl = lax.axis_size("x"), lax.axis_size("zh"), lax.axis_size("zl")
    ny, nc = lax.axis_size("y"), lax.axis_size("core")
    nz = nh * nl
    experts = nx * nz
    cap = min(tok, max(2, 2 * tok * top // experts))
    held = nh * tok
    dests = nx * nl
    per = nh * cap
    slots = dests * per
    nblock = ny * nc
    block = width // nblock

    shift = nl // 2
    groups = [
        [(c * nx + x) * nz + (b * nl + c * shift + l) % nz for x in range(nx) for l in range(nl)]
        for c in range(nc)
        for b in range(nh)
    ]
    core = lax.axis_index("core")
    z = lax.axis_index("zh") * nl + lax.axis_index("zl")
    first = (z - core * shift + nz) % nz // nl * nl + core * shift
    dest = jnp.arange(slots, dtype=jnp.int32) // per
    dest_ids = (dest // nl) * nz + (first + dest % nl) % nz
    dest_ids = dest_ids.astype(F32).reshape(1, slots)
    core_at = core.reshape(1).astype(jnp.int32)

    def forward(a):
        return lax.all_to_all(
            a.reshape(dests, per, -1),
            ("core", "x", "zh", "zl"),
            split_axis=0,
            concat_axis=0,
            tiled=True,
            axis_index_groups=groups,
        ).reshape(slots, -1)

    meta = jnp.concatenate(
        [
            expert_ids.astype(BF),
            route_weights,
            jnp.zeros((tok, META - 2 * top), BF),
        ],
        axis=1,
    )
    packed = jnp.concatenate([tokens, out_grad, meta], axis=1)
    gathered = lax.all_gather(packed, "zh", axis=0, tiled=True)

    send, pick = call(
        functools.partial(select_body, tok, cap, top),
        (
            jax.ShapeDtypeStruct((slots, 2 * width), BF),
            jax.ShapeDtypeStruct((held, slots), BF),
        ),
        4 * slots * held * width,
        6 * slots * width,
    )(gathered, dest_ids)
    came = forward(send)

    gate_w, up_w, down_w = w_gate[0], w_up[0], w_down[0]
    small = jax.ShapeDtypeStruct((slots, ff), BF)
    terms = jax.ShapeDtypeStruct((ny, 3, block, ff), BF)
    smem = pl.BlockSpec(memory_space=pltpu.SMEM)
    hidden, gate_back, up_back, route, other = pl.pallas_call(
        functools.partial(expert_body, nblock),
        out_shape=(small, small, small, jax.ShapeDtypeStruct((slots, META), BF), terms),
        in_specs=[smem] + [VMEM] * 4,
        compiler_params=pltpu.CompilerParams(vmem_limit_bytes=40 * 1024 * 1024),
        cost_estimate=pl.CostEstimate(
            flops=9 * slots * ff * width, bytes_accessed=10_000_000, transcendentals=slots * ff
        ),
    )(core_at, came, gate_w, up_w, down_w)
    arrived = lax.ppermute(other, "core", [(0, 1), (1, 0)])
    back = call(
        back_body,
        jax.ShapeDtypeStruct((slots, width + META), BF),
        4 * slots * ff * width,
        5_000_000,
    )(gate_back, up_back, route, gate_w, up_w)
    pair = pl.pallas_call(
        functools.partial(own_body, nblock),
        out_shape=terms,
        in_specs=[smem] + [VMEM] * 5,
        compiler_params=pltpu.CompilerParams(vmem_limit_bytes=30 * 1024 * 1024),
        cost_estimate=pl.CostEstimate(
            flops=3 * slots * ff * width, bytes_accessed=7_000_000, transcendentals=0
        ),
    )(core_at, came, hidden, gate_back, up_back, arrived)
    total = lax.psum_scatter(
        pair.reshape(ny * 3 * block, ff), "y", scatter_dimension=0, tiled=True
    )
    total = total.reshape(3, block, ff).astype(F32) * (1.0 / (ny * nc))

    back = forward(back)
    outgoing = call(
        functools.partial(combine_body, top),
        jax.ShapeDtypeStruct((held, width + META), BF),
        2 * slots * held * width,
        2_000_000,
    )(back, pick, gathered[:, 2 * width :], dest_ids)
    parts = lax.all_to_all(
        outgoing.reshape(nh, tok, -1), "zh", split_axis=0, concat_axis=0, tiled=True
    )
    summed = jnp.sum(parts.astype(F32), axis=0)
    grad_tokens = summed[:, :width].astype(BF)
    grad_route = summed[:, width : width + top].astype(BF)
    return (grad_tokens, grad_route, total[0][None], total[1][None], total[2].T[None])


def solution(mesh):
    groups, experts = mesh.devices.shape
    n = round(experts ** (1 / 3))
    fine = Mesh(
        mesh.devices.reshape(groups // 2, 2, n, n, n), ("y", "core", "x", "zh", "zl")
    )
    dp = ("y", "core")
    ex = ("x", "zh", "zl")
    rows = P(dp + ex, None)
    return jax.shard_map(
        shards,
        mesh=fine,
        in_specs=(rows, rows, rows, rows) + (P(ex, None, None),) * 3,
        out_specs=(rows, rows, P(ex, dp, None), P(ex, dp, None), P(ex, None, dp)),
        check_vma=False,
    )
```

time: 206 us -> 174 us (0.84); the launches traced: 206 us -> 171 us
  waiting for transfers between devices: 73.3 us -> 12.7 us
  blocking collectives: 57.6 us -> 113 us
  starting transfers between devices: 26.1 us -> 8.82 us
  matrix products: 14.6 us -> 0 us
  Pallas kernels: 0 us -> 10 us
  other arithmetic: 8.05 us -> 1.76 us
  local copies, waits for them, and re-layouts: 12 us -> 9.73 us
    all_to_all x3 -> x1, waiting for transfers between devices: 73.2 us -> 12.7 us  [forward(): lax.all_to_all(a.reshape(dests, per, -1), ('core', 'x', 'zh', 'zl'), spli...]
    all_to_all x0 -> x1, blocking collectives: none -> 52.7 us  [forward(): lax.all_to_all(a.reshape(dests, per, -1), ('core', 'x', 'zh', 'zl'), spli...]
    all_to_all x3 -> x1, starting transfers between devices: 22.4 us -> 6.88 us  [forward(): lax.all_to_all(a.reshape(dests, per, -1), ('core', 'x', 'zh', 'zl'), spli...]
    dot_general x12 -> x0, matrix products: 14.6 us -> none  [the longest x1 2.69 us: shards(): lax.dot_general(scaled, down_w, LAST, preferred_element_type=F32)]
    pallas_call x0 -> x5, Pallas kernels: none -> 10 us  [the longest x1 4.29 us: shards(): pl.pallas_call(functools.partial(expert_body, nblock), out_shape=(small,...]
    convert_element_type x6 -> x1, other arithmetic: 4.8 us -> 0.03 us  [shards(): dest_ids = dest_ids.astype(F32).reshape(1, slots)]
    all_to_all x1, blocking collectives: 24.3 us -> 27.5 us  [shards(): lax.all_to_all(outgoing.reshape(nh, tok, -1), 'zh', split_axis=0, concat_...]
    unnamed x10 -> x23, local copies, waits for them, and re-layouts: 4.79 us -> 6.53 us
  transfers between devices with their start and end apart: 5 -> 3, of which waited for: 3 -> 1; matrix products, arithmetic and copies ran while one was open for 8% -> 1% of each run, Pallas kernels for 0% -> 3%
where the time goes in v2:
time: 174 us; the launch traced here: 171 us
  blocking collectives  113 us (65%)
  between operations  14.2 us (8%)
  waiting for transfers between devices  12.7 us (7%)
  Pallas kernels  10 us (6%)
  local copies, waits for them, and re-layouts  9.73 us (6%)
  starting transfers between devices  8.82 us (5%)
  other arithmetic  1.76 us (1%)
    all_to_all x1, blocking collectives, forward(): lax.all_to_all(a.reshape(dests, per, -1), ('core', 'x', 'zh', 'zl'), spli...  52.7 us
    all_gather x1, blocking collectives, shards(): gathered = lax.all_gather(packed, 'zh', axis=0, tiled=True)  33.3 us
    all_to_all x1, blocking collectives, shards(): lax.all_to_all(outgoing.reshape(nh, tok, -1), 'zh', split_axis=0, concat_...  27.5 us
    all_to_all x1, waiting for transfers between devices, forward(): lax.all_to_all(a.reshape(dests, per, -1), ('core', 'x', 'zh', 'zl'), spli...  12.7 us
    all_to_all x1, starting transfers between devices, forward(): lax.all_to_all(a.reshape(dests, per, -1), ('core', 'x', 'zh', 'zl'), spli...  6.88 us
    unnamed x23, local copies, waits for them, and re-layouts  6.53 us
    pallas_call x1, Pallas kernels, shards(): pl.pallas_call(functools.partial(expert_body, nblock), out_shape=(small,...  4.29 us
  transfers between devices with their start and end apart: 3, of which 1 were waited for; matrix products, arithmetic and copies ran while one was open for 1% of the time, Pallas kernels for 3%

profile of v2, /device:TPU:1, one launch (start us, length us, event | category | flops | bytes accessed | tf_op | source)
XLA Modules:
  0.0 170.7 jit_solution(15936256586518450071)
XLA Ops:
  7.2 0.7 convert_element_type.22
  7.9 0.1 copy.24
  8.0 0.8 copy.25
  8.8 1.0 concatenate.3
  9.7 33.3 %all_gather.3.held_ref = bf16[64,4224]{1,0:T(8,128)(2,1)S(1)} all-gather(bf16[16,4224]{1,0:T(8,128)(2,1)S(1)} %concatenate.3), channel_id=1, replica_groups=mesh['y'=8,'core'=2,'x'=4,'zh'=4,'zl'=4] {'zh'}, dimensions={0}, use_global_device_ids=true | all-gather | bytes 675840 | tf_op jit(solution)/shard_map/all_gather | solution.py:180
  43.0 0.0 copy-start.4
  43.0 0.0 copy-start.5
  43.0 1.0 shard_map.110
  44.1 0.0 copy-start.1
  44.1 0.0 copy-start.2
  44.1 52.7 %all_to_all.15 = bf16[16,16,4096]{2,1,0:T(8,128)(2,1)S(1)} all-to-all(bf16[16,16,4096]{2,1,0:T(8,128)(2,1)S(1)} %bitcast.27), channel_id=1, replica_groups={{0,1,2,3,16,17,18,19,32,33,34,35,48,49,50,51},{4,5,6,7,20,21,22,23,36,3..., dimensions={0} | all-to-all | bytes 4194304 | tf_op jit(solution)/shard_map/all_to_all | solution.py:162
  96.8 0.0 copy-done.4
  96.8 0.0 copy-done.5
  96.8 0.0 copy-done.1
  96.8 0.0 copy-done.2
  96.8 4.3 %shard_map.111 = (bf16[256,384]{1,0:T(8,128)(2,1)S(1)}, bf16[256,384]{1,0:T(8,128)(2,1)S(1)}, bf16[256,384]{1,0:T(8,128)(2,1)S(1)}, bf16[256,128]{1,0:T(8,128)(2,1)S(1)}, bf16[8,3,128,384]{3,2,1,0:T(8,128)(2,1)}) custom-call(s32[1]{0:T(128)} %bitcast.core_ref, bf16[256,4096]{1,0:T(8,128)(2,1)S(1)} %bitcast.18, bf16[2048,384]{1,0:T(8,128)(2,1)S(1)} %bitcast.21, ...), custom_call_target="tpu_custom_call" | custom-call | flops 1811939328 | bytes 10000000 | tf_op jit(solution)/shard_map/pallas_call | solution.py:197
  101.1 0.0 copy-start.6
  101.1 0.0 copy-start.8
  101.1 1.9 %collective-permute-start = (bf16[8,3,128,384]{3,2,1,0:T(8,128)(2,1)}, bf16[8,3,128,384]{3,2,1,0:T(8,128)(2,1)}, u32[]{:S(2)}, u32[]{:S(2)}) collective-permute-start(bf16[8,3,128,384]{3,2,1,0:T(8,128)(2,1)} %get-tuple-element.18), channel_id=1, source_target_pairs={{0,64},{64,0},{1,65},{65,1},{2,66},{66,2},{3,67},{67,3},{4,68},{68... | collective-permute-start | bytes 7077896 | tf_op jit(solution)/shard_map/ppermute | solution.py:206
  103.0 1.3 shard_map.112
  104.3 0.0 copy-done.6
  104.4 0.0 copy-done.8
  104.4 0.0 copy-start.3
  104.4 1.0 copy-done.3
  105.4 6.9 %all-to-all-start.1 = ((bf16[16,16,2176]{2,1,0:T(8,128)(2,1)}), bf16[16,16,2176]{2,1,0:T(8,128)(2,1)S(1)}, u32[]{:S(2)}, u32[]{:S(2)}) async-start(bf16[16,16,2176]{2,1,0:T(8,128)(2,1)} %bitcast.26), calls=%async_computation.1 | async-start | bytes 2228224 | tf_op jit(solution)/shard_map/all_to_all | solution.py:162
  112.3 0.0 reduce-scatter.2.cloned.1.call-start
  112.3 0.0 collective-permute-done.add_ref
  112.3 0.0 copy-start.7
  112.3 0.9 copy-done.7
  113.3 0.0 copy-start.9
  113.3 0.9 copy-done.9
  114.2 2.7 %shard_map.114 = bf16[8,3,128,384]{3,2,1,0:T(8,128)(2,1)S(1)} custom-call(s32[1]{0:T(128)} %bitcast.core_ref, bf16[256,4096]{1,0:T(8,128)(2,1)S(1)} %bitcast.19, bf16[256,384]{1,0:T(8,128)(2,1)S(1)} %copy-done.9, bf16[256,384]{1,0:T(8,128)(2,1)S(1)} %get-tuple-element.13.gate_back_ref, bf16[256,384]{1,0:T(8,128)(2,1)S(1)} %copy-done.7, ...), custom_call_target="tpu_custom_call" | custom-call | flops 603979776 | bytes 7000000 | tf_op jit(solution)/shard_map/pallas_call | solution.py:213
  116.9 0.0 copy-start
  117.0 1.4 copy-done
  118.4 0.0 reduce-scatter.2.cloned.1.call-update
  118.4 0.7 slice.35.meta_ref
  119.1 12.7 %all-to-all-done.1 = bf16[16,16,2176]{2,1,0:T(8,128)(2,1)S(1)} async-done(((bf16[16,16,2176]{2,1,0:T(8,128)(2,1)}), bf16[16,16,2176]{2,1,0:T(8,128)(2,1)S(1)}, u32[]{:S(2)}, u32[]{:S(2)}) %all-to-all-start.1) | async-done | bytes 1114144 | tf_op jit(solution)/shard_map/all_to_all | solution.py:162
  131.8 0.6 shard_map.113
  132.4 27.5 %all_to_all.16 = bf16[4,16,2176]{2,1,0:T(8,128)(2,1)S(1)} all-to-all(bf16[4,16,2176]{2,1,0:T(8,128)(2,1)S(1)} %bitcast.29), channel_id=1, replica_groups=mesh['y'=8,'core'=2,'x'=4,'zh'=4,'zl'=4] {'zh'}, dimensions={0} | all-to-all | bytes 557056 | tf_op jit(solution)/shard_map/all_to_all | solution.py:234
  159.9 0.6 slice.36
  160.6 0.7 copy.26
  161.2 0.0 reduce-scatter.2.cloned.1.call-done
  161.2 1.0 convert_multiply_fusion
  162.2 0.8 slice_bitcast_fusion
  163.0 0.8 copy.27
  (4 shorter events, 0.1 us)
Async XLA Ops:
  43.0 53.8 %copy-start.4 = (bf16[64,4224]{1,0:T(8,128)(2,1)}, bf16[64,4224]{1,0:T(8,128)(2,1)S(1)}, u32[]{:S(2)}) copy-start(bf16[64,4224]{1,0:T(8,128)(2,1)S(1)} %all_gather.3.held_ref) | copy-start | bytes 1622020
  43.0 53.8 %copy-start.5 = (bf16[1,384,2048]{2,1,0:T(8,128)(2,1)S(1)}, bf16[1,384,2048]{2,1,0:T(8,128)(2,1)}, u32[]{:S(2)}) copy-start(bf16[1,384,2048]{2,1,0:T(8,128)(2,1)} %param.13) | copy-start | bytes 4718596
  44.1 52.7 %copy-start.1 = (bf16[1,2048,384]{2,1,0:T(8,128)(2,1)S(1)}, bf16[1,2048,384]{2,1,0:T(8,128)(2,1)}, u32[]{:S(2)}) copy-start(bf16[1,2048,384]{2,1,0:T(8,128)(2,1)} %param.11) | copy-start | bytes 4718596
  44.1 52.7 %copy-start.2 = (bf16[1,2048,384]{2,1,0:T(8,128)(2,1)S(1)}, bf16[1,2048,384]{2,1,0:T(8,128)(2,1)}, u32[]{:S(2)}) copy-start(bf16[1,2048,384]{2,1,0:T(8,128)(2,1)} %param.12) | copy-start | bytes 4718596
  101.1 3.2 %copy-start.6 = (bf16[256,384]{1,0:T(8,128)(2,1)}, bf16[256,384]{1,0:T(8,128)(2,1)S(1)}, u32[]{:S(2)}) copy-start(bf16[256,384]{1,0:T(8,128)(2,1)S(1)} %get-tuple-element.14.up_back_ref) | copy-start | bytes 589828
  101.1 3.2 %copy-start.8 = (bf16[256,384]{1,0:T(8,128)(2,1)}, bf16[256,384]{1,0:T(8,128)(2,1)S(1)}, u32[]{:S(2)}) copy-start(bf16[256,384]{1,0:T(8,128)(2,1)S(1)} %get-tuple-element.17.hidden_ref) | copy-start | bytes 589828
  101.1 11.2 %collective-permute-start = (bf16[8,3,128,384]{3,2,1,0:T(8,128)(2,1)}, bf16[8,3,128,384]{3,2,1,0:T(8,128)(2,1)}, u32[]{:S(2)}, u32[]{:S(2)}) collective-permute-start(bf16[8,3,128,384]{3,2,1,0:T(8,128)(2,1)} %get-tuple-element.18), channel_id=1, source_target_pairs={{0,64},{64,0},{1,65},{65,1},{2,66},{66,2},{3,67},{67,3},{4,68},{68... | collective-permute-start | bytes 7077896 | tf_op jit(solution)/shard_map/ppermute | solution.py:206
  104.4 1.0 copy-start.3
  105.4 26.4 %all-to-all-start.1 = ((bf16[16,16,2176]{2,1,0:T(8,128)(2,1)}), bf16[16,16,2176]{2,1,0:T(8,128)(2,1)S(1)}, u32[]{:S(2)}, u32[]{:S(2)}) async-start(bf16[16,16,2176]{2,1,0:T(8,128)(2,1)} %bitcast.26), calls=%async_computation.1 | async-start | bytes 2228224 | tf_op jit(solution)/shard_map/all_to_all | solution.py:162
  112.3 49.0 %reduce-scatter.2.cloned.1.call-start = ((), (), s32[]{:S(2)}) async-start(), calls=%async_computation.4 | async-start | bytes 2654208 | tf_op jit(solution)/shard_map/reduce_scatter | solution.py:222
  112.3 0.9 copy-start.7
  113.3 0.9 copy-start.9
  116.9 1.4 copy-start
Sparse Core Ops, SparseCore 0:
  118.5 42.5 reduce-scatter.1

commit v3 on v2

--- a/solution.py
+++ b/solution.py
@@ -12,22 +12,64 @@
 F32 = jnp.float32
 META = 128
 VMEM = pl.BlockSpec(memory_space=pltpu.VMEM)
+APART = pl.BlockSpec(memory_space=pltpu.HBM)
 FIRST = (((0,), (0,)), ((), ()))
 LAST = (((1,), (1,)), ((), ()))
 
 
-def call(body, outs, flops, moved):
+def call(body, outs, flops, moved, ins=None, scratch=(), limit=16, exps=0, out_specs=None):
+    extra = {} if ins is None else {"in_specs": ins}
+    if out_specs is not None:
+        extra["out_specs"] = out_specs
     return pl.pallas_call(
         body,
         out_shape=outs,
-        compiler_params=pltpu.CompilerParams(vmem_limit_bytes=30 * 1024 * 1024),
-        cost_estimate=pl.CostEstimate(flops=flops, bytes_accessed=moved, transcendentals=0),
-    )
-
-
-def select_body(tok, cap, top, held_ref, dest_ref, send_ref, pick_ref):
+        scratch_shapes=scratch,
+        compiler_params=pltpu.CompilerParams(vmem_limit_bytes=limit * 1024 * 1024),
+        cost_estimate=pl.CostEstimate(flops=flops, bytes_accessed=moved, transcendentals=exps),
+        **extra,
+    )
+
+
+def pack_body(top, tokens_ref, cots_ref, ids_ref, weights_ref, out_ref, ids_here, weights_here, sems):
+    width = tokens_ref.shape[1]
+    copies = [
+        pltpu.make_async_copy(source, target, sems.at[n])
+        for n, (source, target) in enumerate(
+            (
+                (ids_ref, ids_here),
+                (weights_ref, weights_here),
+                (tokens_ref, out_ref.at[:, pl.ds(0, width)]),
+                (cots_ref, out_ref.at[:, pl.ds(width, width)]),
+            )
+        )
+    ]
+    for copy in copies:
+        copy.start()
+    lane = lax.broadcasted_iota(jnp.int32, (top, META), 1)
+    row = lax.broadcasted_iota(jnp.int32, (top, META), 0)
+    copies[0].wait()
+    copies[1].wait()
+    meta = lax.dot_general(
+        ids_here[...].astype(F32).astype(BF),
+        jnp.where(lane == row, 1.0, 0.0).astype(BF),
+        FIRST,
+        preferred_element_type=F32,
+    ) + lax.dot_general(
+        weights_here[...].astype(F32).astype(BF),
+        jnp.where(lane == row + top, 1.0, 0.0).astype(BF),
+        FIRST,
+        preferred_element_type=F32,
+    )
+    out_ref[:, 2 * width :] = meta.astype(BF)
+    copies[2].wait()
+    copies[3].wait()
+
+
+def select_body(tok, cap, top, held_ref, dest_ref, send_ref, pick_ref, meta_ref):
     held = held_ref.shape[0]
     slots, width = send_ref.shape[0], send_ref.shape[1] // 2
+    meta_ref[...] = held_ref[:, 2 * width :]
     meta = held_ref[:, 2 * width :].astype(F32)
     dest = dest_ref[...]
     match = jnp.zeros((held, slots), F32)
@@ -55,7 +97,21 @@
         ).astype(BF)
 
 
-def expert_body(nblock, core_ref, came_ref, gate_ref, up_ref, down_ref, hidden_ref, gate_back_ref, up_back_ref, route_ref, other_ref):
+def expert_body(
+    nblock,
+    core_ref,
+    came_ref,
+    gate_ref,
+    up_ref,
+    down_ref,
+    hidden_ref,
+    gate_back_ref,
+    up_back_ref,
+    route_ref,
+    other_ref,
+    buffer,
+    sems,
+):
     width = came_ref.shape[1] // 2
     inputs, scaled = came_ref[:, :width], came_ref[:, width:]
     pre_gate = jnp.dot(inputs, gate_ref[...], preferred_element_type=F32)
@@ -75,29 +131,78 @@
     route_ref[...] = jnp.where(
         lane == 0, high, jnp.where(lane == 1, route - high, 0.0)
     ).astype(BF)
-    weight_terms(nblock, 1 - core_ref[0], came_ref, hidden, gate_back, up_back, None, other_ref)
-
-
-def weight_terms(nblock, core, came_ref, hidden, gate_back, up_back, add_ref, out_ref):
+    copies = []
+    for y in range(nblock // 2):
+        weight_terms(nblock, y, 1 - core_ref[0], came_ref, hidden, gate_back, up_back, buffer)
+        copies.append(pltpu.make_async_copy(buffer.at[y], other_ref.at[y], sems.at[y]))
+        copies[-1].start()
+    for copy in copies:
+        copy.wait()
+
+
+def weight_terms(nblock, y, core, came_ref, hidden, gate_back, up_back, out_ref):
     width = came_ref.shape[1] // 2
     block = width // nblock
+    for which, (base, right) in enumerate(((0, gate_back), (0, up_back), (width, hidden))):
+        at = pl.multiple_of(base + (2 * y + core) * block, block)
+        out_ref[y, which] = lax.dot_general(
+            came_ref[:, pl.ds(at, block)], right, FIRST, preferred_element_type=F32
+        ).astype(BF)
+
+
+def own_body(nblock, core_ref, came_ref, hidden_ref, gate_back_ref, up_back_ref, out_ref):
     for y in range(nblock // 2):
-        for which, (base, right) in enumerate(
-            ((0, gate_back), (0, up_back), (width, hidden))
-        ):
-            at = pl.multiple_of(base + (2 * y + core) * block, block)
-            term = lax.dot_general(
-                came_ref[:, pl.ds(at, block)], right, FIRST, preferred_element_type=F32
-            )
-            if add_ref is not None:
-                term = term + add_ref[y, which].astype(F32)
-            out_ref[y, which] = term.astype(BF)
-
-
-def own_body(nblock, core_ref, came_ref, hidden_ref, gate_back_ref, up_back_ref, add_ref, out_ref):
-    weight_terms(
-        nblock, core_ref[0], came_ref, hidden_ref[...], gate_back_ref[...], up_back_ref[...], add_ref, out_ref
-    )
+        weight_terms(
+            nblock,
+            y,
+            core_ref[0],
+            came_ref,
+            hidden_ref[...],
+            gate_back_ref[...],
+            up_back_ref[...],
+            out_ref,
+        )
+
+
+def add_body(own_ref, arrived_ref, out_ref, came, went, in_sems, out_sems):
+    steps = own_ref.shape[0]
+    reads = [
+        pltpu.make_async_copy(arrived_ref.at[y], came.at[y], in_sems.at[y]) for y in range(steps)
+    ]
+    writes = [
+        pltpu.make_async_copy(went.at[y], out_ref.at[y], out_sems.at[y]) for y in range(steps)
+    ]
+    for read in reads:
+        read.start()
+    for y in range(steps):
+        reads[y].wait()
+        went[y] = (own_ref[y].astype(F32) + came[y].astype(F32)).astype(BF)
+        writes[y].start()
+    for write in writes:
+        write.wait()
+
+
+def final_body(scale, total_ref, gate_ref, up_ref, down_ref):
+    block = gate_ref.shape[0]
+    gate_ref[...] = total_ref[:block].astype(F32) * scale
+    up_ref[...] = total_ref[block : 2 * block].astype(F32) * scale
+    down_ref[...] = (total_ref[2 * block :].astype(F32) * scale).T
+
+
+def sum_body(top, parts_ref, tokens_ref, route_ref):
+    width = tokens_ref.shape[1]
+    total = parts_ref[0].astype(F32)
+    for h in range(1, parts_ref.shape[0]):
+        total = total + parts_ref[h].astype(F32)
+    tokens_ref[...] = total[:, :width].astype(BF)
+    lane = lax.broadcasted_iota(jnp.int32, (top, META), 1)
+    row = lax.broadcasted_iota(jnp.int32, (top, META), 0)
+    route_ref[...] = lax.dot_general(
+        jnp.where(lane == row, 1.0, 0.0).astype(BF),
+        total[:, width:].astype(BF),
+        LAST,
+        preferred_element_type=F32,
+    ).astype(BF)
 
 
 def back_body(gate_back_ref, up_back_ref, route_ref, gate_ref, up_ref, out_ref):
@@ -168,22 +273,28 @@
             axis_index_groups=groups,
         ).reshape(slots, -1)
 
-    meta = jnp.concatenate(
-        [
-            expert_ids.astype(BF),
-            route_weights,
-            jnp.zeros((tok, META - 2 * top), BF),
+    packed = call(
+        functools.partial(pack_body, top),
+        jax.ShapeDtypeStruct((tok, 2 * width + META), BF),
+        0,
+        4 * tok * width,
+        ins=[APART] * 4,
+        out_specs=VMEM,
+        scratch=[
+            pltpu.VMEM((top, tok), jnp.int32),
+            pltpu.VMEM((top, tok), BF),
+            pltpu.SemaphoreType.DMA((4,)),
         ],
-        axis=1,
-    )
-    packed = jnp.concatenate([tokens, out_grad, meta], axis=1)
+        limit=60,
+    )(tokens, out_grad, expert_ids.T, route_weights.T)
     gathered = lax.all_gather(packed, "zh", axis=0, tiled=True)
 
-    send, pick = call(
+    send, pick, meta = call(
         functools.partial(select_body, tok, cap, top),
         (
             jax.ShapeDtypeStruct((slots, 2 * width), BF),
             jax.ShapeDtypeStruct((held, slots), BF),
+            jax.ShapeDtypeStruct((held, META), BF),
         ),
         4 * slots * held * width,
         6 * slots * width,
@@ -192,16 +303,19 @@
 
     gate_w, up_w, down_w = w_gate[0], w_up[0], w_down[0]
     small = jax.ShapeDtypeStruct((slots, ff), BF)
-    terms = jax.ShapeDtypeStruct((ny, 3, block, ff), BF)
+    shape = (ny, 3, block, ff)
+    terms = jax.ShapeDtypeStruct(shape, BF)
     smem = pl.BlockSpec(memory_space=pltpu.SMEM)
-    hidden, gate_back, up_back, route, other = pl.pallas_call(
+    hidden, gate_back, up_back, route, other = call(
         functools.partial(expert_body, nblock),
-        out_shape=(small, small, small, jax.ShapeDtypeStruct((slots, META), BF), terms),
-        in_specs=[smem] + [VMEM] * 4,
-        compiler_params=pltpu.CompilerParams(vmem_limit_bytes=40 * 1024 * 1024),
-        cost_estimate=pl.CostEstimate(
-            flops=9 * slots * ff * width, bytes_accessed=10_000_000, transcendentals=slots * ff
-        ),
+        (small, small, small, jax.ShapeDtypeStruct((slots, META), BF), terms),
+        9 * slots * ff * width,
+        10_000_000,
+        ins=[smem] + [VMEM] * 4,
+        out_specs=(VMEM,) * 4 + (APART,),
+        scratch=[pltpu.VMEM(shape, BF), pltpu.SemaphoreType.DMA((ny,))],
+        limit=28,
+        exps=slots * ff,
     )(core_at, came, gate_w, up_w, down_w)
     arrived = lax.ppermute(other, "core", [(0, 1), (1, 0)])
     back = call(
@@ -210,19 +324,41 @@
         4 * slots * ff * width,
         5_000_000,
     )(gate_back, up_back, route, gate_w, up_w)
-    pair = pl.pallas_call(
+    own = call(
         functools.partial(own_body, nblock),
-        out_shape=terms,
-        in_specs=[smem] + [VMEM] * 5,
-        compiler_params=pltpu.CompilerParams(vmem_limit_bytes=30 * 1024 * 1024),
-        cost_estimate=pl.CostEstimate(
-            flops=3 * slots * ff * width, bytes_accessed=7_000_000, transcendentals=0
-        ),
-    )(core_at, came, hidden, gate_back, up_back, arrived)
+        terms,
+        3 * slots * ff * width,
+        5_000_000,
+        ins=[smem] + [VMEM] * 4,
+    )(core_at, came, hidden, gate_back, up_back)
+    pair = call(
+        add_body,
+        terms,
+        0,
+        7_000_000,
+        ins=[VMEM, APART],
+        out_specs=APART,
+        scratch=[
+            pltpu.VMEM(shape, BF),
+            pltpu.VMEM(shape, BF),
+            pltpu.SemaphoreType.DMA((ny,)),
+            pltpu.SemaphoreType.DMA((ny,)),
+        ],
+    )(own, arrived)
+    pair, back = lax.optimization_barrier((pair, back))
     total = lax.psum_scatter(
         pair.reshape(ny * 3 * block, ff), "y", scatter_dimension=0, tiled=True
     )
-    total = total.reshape(3, block, ff).astype(F32) * (1.0 / (ny * nc))
+    grads = call(
+        functools.partial(final_body, 1.0 / nblock),
+        (
+            jax.ShapeDtypeStruct((block, ff), F32),
+            jax.ShapeDtypeStruct((block, ff), F32),
+            jax.ShapeDtypeStruct((ff, block), F32),
+        ),
+        0,
+        9 * block * ff,
+    )(total)
 
     back = forward(back)
     outgoing = call(
@@ -230,14 +366,17 @@
         jax.ShapeDtypeStruct((held, width + META), BF),
         2 * slots * held * width,
         2_000_000,
-    )(back, pick, gathered[:, 2 * width :], dest_ids)
+    )(back, pick, meta, dest_ids)
     parts = lax.all_to_all(
         outgoing.reshape(nh, tok, -1), "zh", split_axis=0, concat_axis=0, tiled=True
     )
-    summed = jnp.sum(parts.astype(F32), axis=0)
-    grad_tokens = summed[:, :width].astype(BF)
-    grad_route = summed[:, width : width + top].astype(BF)
-    return (grad_tokens, grad_route, total[0][None], total[1][None], total[2].T[None])
+    grad_tokens, grad_route = call(
+        functools.partial(sum_body, top),
+        (jax.ShapeDtypeStruct((tok, width), BF), jax.ShapeDtypeStruct((top, tok), BF)),
+        0,
+        10 * tok * width,
+    )(parts)
+    return (grad_tokens, grad_route.T) + tuple(g[None] for g in grads)
 
 
 def solution(mesh):

time: 174 us -> 176 us (1.011)
  waiting for transfers between devices: 12.7 us -> 40.5 us
  blocking collectives: 113 us -> 86.2 us
  local copies, waits for them, and re-layouts: 9.73 us -> 0.98 us
  starting transfers between devices: 8.82 us -> 14.9 us
  Pallas kernels: 10 us -> 15.8 us
    all_to_all x1 -> x0, blocking collectives: 27.5 us -> none  [shards(): lax.all_to_all(outgoing.reshape(nh, tok, -1), 'zh', split_axis=0, concat_...]
    reduce_scatter x1, waiting for transfers between devices: 0.01 us -> 19.9 us  [shards(): lax.psum_scatter(pair.reshape(ny * 3 * block, ff), 'y', scatter_dimension...]
    all_to_all x0 -> x1, starting transfers between devices: none -> 6.16 us  [shards(): lax.all_to_all(outgoing.reshape(nh, tok, -1), 'zh', split_axis=0, concat_...]
    all_to_all x1, waiting for transfers between devices: 12.7 us -> 18.8 us  [forward(): lax.all_to_all(a.reshape(dests, per, -1), ('core', 'x', 'zh', 'zl'), spli...]
    unnamed x23 -> x8, local copies, waits for them, and re-layouts: 6.53 us -> 0.98 us
    pallas_call x2 -> x6, Pallas kernels: 7.04 us -> 11.2 us  [the longest x1 4.81 us: shards(): call(functools.partial(expert_body, nblock), (small, small, small, jax.Sh...]
  transfers between devices with their start and end apart: 3 -> 4, of which waited for: 1 -> 3; matrix products, arithmetic and copies ran while one was open for 1% -> 0% of each run, Pallas kernels for 3% -> 3%
where the time goes in v3:
time: 176 us; the launch traced here: 173 us
  blocking collectives  86.2 us (49%)
  waiting for transfers between devices  40.5 us (23%)
  Pallas kernels  15.8 us (9%)
  starting transfers between devices  14.9 us (8%)
  between operations  14.1 us (8%)
    all_to_all x1, blocking collectives, forward(): lax.all_to_all(a.reshape(dests, per, -1), ('core', 'x', 'zh', 'zl'), spli...  52.7 us
    all_gather x1, blocking collectives, shards(): gathered = lax.all_gather(packed, 'zh', axis=0, tiled=True)  33.5 us
    reduce_scatter x1, waiting for transfers between devices, shards(): lax.psum_scatter(pair.reshape(ny * 3 * block, ff), 'y', scatter_dimension...  19.9 us
    all_to_all x1, waiting for transfers between devices, forward(): lax.all_to_all(a.reshape(dests, per, -1), ('core', 'x', 'zh', 'zl'), spli...  18.8 us
    all_to_all x1, starting transfers between devices, forward(): lax.all_to_all(a.reshape(dests, per, -1), ('core', 'x', 'zh', 'zl'), spli...  6.79 us
    all_to_all x1, starting transfers between devices, shards(): lax.all_to_all(outgoing.reshape(nh, tok, -1), 'zh', split_axis=0, concat_...  6.16 us
    pallas_call x1, Pallas kernels, shards(): call(functools.partial(expert_body, nblock), (small, small, small, jax.Sh...  4.81 us
  transfers between devices with their start and end apart: 4, of which 3 were waited for; matrix products, arithmetic and copies ran while one was open for 0% of the time, Pallas kernels for 3%

profile of v3, /device:TPU:1, one launch (start us, length us, event | category | flops | bytes accessed | tf_op | source)
XLA Modules:
  0.0 172.6 jit_solution(2610815384430204543)
XLA Ops:
  7.2 1.6 shard_map.110
  8.8 33.5 %all_gather.3.held_ref = bf16[64,4224]{1,0:T(8,128)(2,1)S(1)} all-gather(bf16[16,4224]{1,0:T(8,128)(2,1)} %shard_map.110), channel_id=1, replica_groups=mesh['y'=8,'core'=2,'x'=4,'zh'=4,'zl'=4] {'zh'}, dimensions={0}, use_global_device_ids=true | all-gather | bytes 675840 | tf_op jit(solution)/shard_map/all_gather | solution.py:290
  42.3 0.0 copy-start.2
  42.3 1.0 shard_map.111
  43.4 0.0 copy-start
  43.4 0.0 copy-start.1
  43.4 52.7 %all_to_all.15 = bf16[16,16,4096]{2,1,0:T(8,128)(2,1)S(1)} all-to-all(bf16[16,16,4096]{2,1,0:T(8,128)(2,1)S(1)} %bitcast.23), channel_id=1, replica_groups={{0,1,2,3,16,17,18,19,32,33,34,35,48,49,50,51},{4,5,6,7,20,21,22,23,36,3..., dimensions={0} | all-to-all | bytes 4194304 | tf_op jit(solution)/shard_map/all_to_all | solution.py:267
  96.1 0.0 copy-done.2
  96.1 0.0 copy-done
  96.1 0.0 copy-done.1
  96.1 4.8 %shard_map.112 = (bf16[256,384]{1,0:T(8,128)(2,1)S(1)}, bf16[256,384]{1,0:T(8,128)(2,1)S(1)}, bf16[256,384]{1,0:T(8,128)(2,1)S(1)}, bf16[256,128]{1,0:T(8,128)(2,1)S(1)}, bf16[8,3,128,384]{3,2,1,0:T(8,128)(2,1)S(1)}) custom-call(s32[1]{0:T(128)} %bitcast.core_ref, bf16[256,4096]{1,0:T(8,128)(2,1)S(1)} %bitcast.16, bf16[2048,384]{1,0:T(8,128)(2,1)S(1)} %bitcast.18, ...), custom_call_target="tpu_custom_call" | custom-call | flops 1811939328 | bytes 10000000 | tf_op jit(solution)/shard_map/pallas_call | solution.py:309
  100.9 1.9 %collective-permute-start = (bf16[8,3,128,384]{3,2,1,0:T(8,128)(2,1)S(1)}, bf16[8,3,128,384]{3,2,1,0:T(8,128)(2,1)S(1)}, u32[]{:S(2)}, u32[]{:S(2)}) collective-permute-start(bf16[8,3,128,384]{3,2,1,0:T(8,128)(2,1)S(1)} %get-tuple-element.24), channel_id=1, source_target_pairs={{0,64},{64,0},{1,65},{65,1},{2,66},{66,2},{3,67},{67,3},{4,68},{68... | collective-permute-start | bytes 7077896 | tf_op jit(solution)/shard_map/ppermute | solution.py:320
  102.9 1.1 shard_map.113.own_ref
  103.9 2.3 %shard_map.115 = bf16[256,2176]{1,0:T(8,128)(2,1)} custom-call(bf16[256,384]{1,0:T(8,128)(2,1)S(1)} %get-tuple-element.22.gate_back_ref, bf16[256,384]{1,0:T(8,128)(2,1)S(1)} %get-tuple-element.23.up_back_ref, bf16[256,128]{1,0:T(8,128)(2,1)S(1)} %get-tuple-element.25.route_ref, bf16[2048,384]{1,0:T(8,128)(2,1)S(1)} %bitcast.19, bf16[2048,384]{1,0:T(8,128)(2,1)S(1)} %bitcast.21), custom_call_target="tpu_custom_call" | custom-call | flops 805306368 | bytes 5000000 | tf_op jit(solution)/shard_map/pallas_call | solution.py:321
  106.2 1.2 collective-permute-done.arrived_ref
  107.4 2.1 %shard_map.114 = bf16[8,3,128,384]{3,2,1,0:T(8,128)(2,1)} custom-call(bf16[8,3,128,384]{3,2,1,0:T(8,128)(2,1)S(1)} %shard_map.113.own_ref, bf16[8,3,128,384]{3,2,1,0:T(8,128)(2,1)S(1)} %collective-permute-done.arrived_ref), custom_call_target="tpu_custom_call" | custom-call | bytes 7000000 | tf_op jit(solution)/shard_map/pallas_call | solution.py:334
  109.5 6.8 %all-to-all-start.1 = ((bf16[16,16,2176]{2,1,0:T(8,128)(2,1)}), bf16[16,16,2176]{2,1,0:T(8,128)(2,1)S(1)}, u32[]{:S(2)}, u32[]{:S(2)}) async-start(bf16[16,16,2176]{2,1,0:T(8,128)(2,1)} %bitcast.8), calls=%async_computation.1 | async-start | bytes 2228224 | tf_op jit(solution)/shard_map/all_to_all | solution.py:267
  116.3 0.0 reduce-scatter.2.cloned.1.call-start
  116.3 0.7 reduce-scatter.2.cloned.1.call-update
  117.0 18.8 %all-to-all-done.1 = bf16[16,16,2176]{2,1,0:T(8,128)(2,1)S(1)} async-done(((bf16[16,16,2176]{2,1,0:T(8,128)(2,1)}), bf16[16,16,2176]{2,1,0:T(8,128)(2,1)S(1)}, u32[]{:S(2)}, u32[]{:S(2)}) %all-to-all-start.1) | async-done | bytes 1114144 | tf_op jit(solution)/shard_map/all_to_all | solution.py:267
  135.8 1.3 shard_map.116
  137.1 6.2 %all-to-all-start.2 = ((bf16[4,16,2176]{2,1,0:T(8,128)(2,1)}), bf16[4,16,2176]{2,1,0:T(8,128)(2,1)S(1)}, u32[]{:S(2)}, u32[]{:S(2)}) async-start(bf16[4,16,2176]{2,1,0:T(8,128)(2,1)} %bitcast.10), calls=%async_computation.2 | async-start | bytes 557056 | tf_op jit(solution)/shard_map/all_to_all | solution.py:370
  143.3 19.9 %reduce-scatter.2.cloned.1.call-done.total_ref = bf16[384,384]{1,0:T(8,128)(2,1)} async-done(((bf16[3072,384]{1,0:T(8,128)(2,1)}), bf16[384,384]{1,0:T(8,128)(2,1)}) %reduce-scatter.2.cloned.1.call-update) | async-done | bytes 294928 | tf_op jit(solution)/shard_map/reduce_scatter | solution.py:349
  163.2 0.0 copy-start.3
  163.2 1.0 copy-done.3
  164.2 0.9 shard_map.118
  165.0 0.0 all-to-all-done.2.parts_ref
  165.0 0.7 shard_map.117
  (1 shorter events, 0.0 us)
Async XLA Ops:
  42.3 53.8 %copy-start.2 = (bf16[1,384,2048]{2,1,0:T(8,128)(2,1)S(1)}, bf16[1,384,2048]{2,1,0:T(8,128)(2,1)}, u32[]{:S(2)}) copy-start(bf16[1,384,2048]{2,1,0:T(8,128)(2,1)} %param.13) | copy-start | bytes 4718596
  43.4 52.7 %copy-start = (bf16[1,2048,384]{2,1,0:T(8,128)(2,1)S(1)}, bf16[1,2048,384]{2,1,0:T(8,128)(2,1)}, u32[]{:S(2)}) copy-start(bf16[1,2048,384]{2,1,0:T(8,128)(2,1)} %param.11) | copy-start | bytes 4718596
  43.4 52.7 %copy-start.1 = (bf16[1,2048,384]{2,1,0:T(8,128)(2,1)S(1)}, bf16[1,2048,384]{2,1,0:T(8,128)(2,1)}, u32[]{:S(2)}) copy-start(bf16[1,2048,384]{2,1,0:T(8,128)(2,1)} %param.12) | copy-start | bytes 4718596
  100.9 6.4 %collective-permute-start = (bf16[8,3,128,384]{3,2,1,0:T(8,128)(2,1)S(1)}, bf16[8,3,128,384]{3,2,1,0:T(8,128)(2,1)S(1)}, u32[]{:S(2)}, u32[]{:S(2)}) collective-permute-start(bf16[8,3,128,384]{3,2,1,0:T(8,128)(2,1)S(1)} %get-tuple-element.24), channel_id=1, source_target_pairs={{0,64},{64,0},{1,65},{65,1},{2,66},{66,2},{3,67},{67,3},{4,68},{68... | collective-permute-start | bytes 7077896 | tf_op jit(solution)/shard_map/ppermute | solution.py:320
  109.5 26.3 %all-to-all-start.1 = ((bf16[16,16,2176]{2,1,0:T(8,128)(2,1)}), bf16[16,16,2176]{2,1,0:T(8,128)(2,1)S(1)}, u32[]{:S(2)}, u32[]{:S(2)}) async-start(bf16[16,16,2176]{2,1,0:T(8,128)(2,1)} %bitcast.8), calls=%async_computation.1 | async-start | bytes 2228224 | tf_op jit(solution)/shard_map/all_to_all | solution.py:267
  116.3 46.9 %reduce-scatter.2.cloned.1.call-start = ((), (), s32[]{:S(2)}) async-start(), calls=%async_computation.4 | async-start | bytes 2654208 | tf_op jit(solution)/shard_map/reduce_scatter | solution.py:349
  137.1 27.9 %all-to-all-start.2 = ((bf16[4,16,2176]{2,1,0:T(8,128)(2,1)}), bf16[4,16,2176]{2,1,0:T(8,128)(2,1)S(1)}, u32[]{:S(2)}, u32[]{:S(2)}) async-start(bf16[4,16,2176]{2,1,0:T(8,128)(2,1)} %bitcast.10), calls=%async_computation.2 | async-start | bytes 557056 | tf_op jit(solution)/shard_map/all_to_all | solution.py:370
  163.2 1.0 copy-start.3
Sparse Core Ops, SparseCore 0:
  120.6 42.5 reduce-scatter.1

commit v4 on v3

--- a/solution.py
+++ b/solution.py
@@ -164,20 +164,12 @@
         )
 
 
-def add_body(own_ref, arrived_ref, out_ref, came, went, in_sems, out_sems):
-    steps = own_ref.shape[0]
-    reads = [
-        pltpu.make_async_copy(arrived_ref.at[y], came.at[y], in_sems.at[y]) for y in range(steps)
-    ]
-    writes = [
-        pltpu.make_async_copy(went.at[y], out_ref.at[y], out_sems.at[y]) for y in range(steps)
-    ]
-    for read in reads:
-        read.start()
-    for y in range(steps):
-        reads[y].wait()
-        went[y] = (own_ref[y].astype(F32) + came[y].astype(F32)).astype(BF)
-        writes[y].start()
+def add_body(own_ref, arrived_ref, out_ref, went, sems):
+    writes = []
+    for y in range(own_ref.shape[0]):
+        went[y] = (own_ref[y].astype(F32) + arrived_ref[y].astype(F32)).astype(BF)
+        writes.append(pltpu.make_async_copy(went.at[y], out_ref.at[y], sems.at[y]))
+        writes[-1].start()
     for write in writes:
         write.wait()
 
@@ -336,14 +328,9 @@
         terms,
         0,
         7_000_000,
-        ins=[VMEM, APART],
+        ins=[VMEM, VMEM],
         out_specs=APART,
-        scratch=[
-            pltpu.VMEM(shape, BF),
-            pltpu.VMEM(shape, BF),
-            pltpu.SemaphoreType.DMA((ny,)),
-            pltpu.SemaphoreType.DMA((ny,)),
-        ],
+        scratch=[pltpu.VMEM(shape, BF), pltpu.SemaphoreType.DMA((ny,))],
     )(own, arrived)
     pair, back = lax.optimization_barrier((pair, back))
     total = lax.psum_scatter(
@@ -360,22 +347,28 @@
         9 * block * ff,
     )(total)
 
-    back = forward(back)
-    outgoing = call(
-        functools.partial(combine_body, top),
-        jax.ShapeDtypeStruct((held, width + META), BF),
-        2 * slots * held * width,
-        2_000_000,
-    )(back, pick, meta, dest_ids)
-    parts = lax.all_to_all(
-        outgoing.reshape(nh, tok, -1), "zh", split_axis=0, concat_axis=0, tiled=True
-    )
-    grad_tokens, grad_route = call(
-        functools.partial(sum_body, top),
-        (jax.ShapeDtypeStruct((tok, width), BF), jax.ShapeDtypeStruct((top, tok), BF)),
-        0,
-        10 * tok * width,
-    )(parts)
+    def way_back(back, pick, meta, dest_ids):
+        back = forward(back)
+        outgoing = call(
+            functools.partial(combine_body, top),
+            jax.ShapeDtypeStruct((held, width + META), BF),
+            2 * slots * held * width,
+            2_000_000,
+        )(back, pick, meta, dest_ids)
+        parts = lax.all_to_all(
+            outgoing.reshape(nh, tok, -1), "zh", split_axis=0, concat_axis=0, tiled=True
+        )
+        grad_tokens, grad_route = call(
+            functools.partial(sum_body, top),
+            (jax.ShapeDtypeStruct((tok, width), BF), jax.ShapeDtypeStruct((top, tok), BF)),
+            0,
+            10 * tok * width,
+        )(parts)
+        return grad_tokens, grad_route
+
+    grad_tokens, grad_route = lax.cond(
+        route_weights[0, 0] > 0, way_back, way_back, back, pick, meta, dest_ids
+    )
     return (grad_tokens, grad_route.T) + tuple(g[None] for g in grads)
 
 

time: 176 us -> 178 us (1.011); the launches traced: 173 us -> 178 us
  blocking collectives: 86.2 us -> 143 us
  waiting for transfers between devices: 40.5 us -> 2.17 us
  starting transfers between devices: 14.9 us -> 1.96 us
  Pallas kernels: 15.8 us -> 13.5 us
    all_to_all x1 -> x2, blocking collectives: 52.7 us -> 81.7 us  [forward(): lax.all_to_all(a.reshape(dests, per, -1), ('core', 'x', 'zh', 'zl'), spli...]
    all_to_all x0 -> x1, blocking collectives: none -> 27.8 us  [way_back(): lax.all_to_all(outgoing.reshape(nh, tok, -1), 'zh', split_axis=0, concat_...]
    reduce_scatter x1, waiting for transfers between devices: 19.9 us -> 0.01 us  [shards(): lax.psum_scatter(pair.reshape(ny * 3 * block, ff), 'y', scatter_dimension...]
    all_to_all x2 -> x0, waiting for transfers between devices: 18.8 us -> none  [the longest x1 18.8 us: forward(): lax.all_to_all(a.reshape(dests, per, -1), ('core', 'x', 'zh', 'zl'), spli...]
    all_to_all x2 -> x0, starting transfers between devices: 12.9 us -> none  [the longest x1 6.79 us: forward(): lax.all_to_all(a.reshape(dests, per, -1), ('core', 'x', 'zh', 'zl'), spli...]
  transfers between devices with their start and end apart: 4 -> 2, of which waited for: 3 -> 1; matrix products, arithmetic and copies ran while one was open for 0% -> 1% of each run, Pallas kernels for 3% -> 2%
where the time goes in v4:
time: 178 us
  blocking collectives  143 us (80%)
  between operations  14.8 us (8%)
  Pallas kernels  13.5 us (8%)
  local copies, waits for them, and re-layouts  2.18 us (1%)
  waiting for transfers between devices  2.17 us (1%)
  starting transfers between devices  1.96 us (1%)
    all_to_all x2, blocking collectives, forward(): lax.all_to_all(a.reshape(dests, per, -1), ('core', 'x', 'zh', 'zl'), spli...  81.7 us
    all_gather x1, blocking collectives, shards(): gathered = lax.all_gather(packed, 'zh', axis=0, tiled=True)  33.5 us
    all_to_all x1, blocking collectives, way_back(): lax.all_to_all(outgoing.reshape(nh, tok, -1), 'zh', split_axis=0, concat_...  27.8 us
    pallas_call x1, Pallas kernels, shards(): call(functools.partial(expert_body, nblock), (small, small, small, jax.Sh...  4.81 us
  transfers between devices with their start and end apart: 2, of which 1 were waited for; matrix products, arithmetic and copies ran while one was open for 1% of the time, Pallas kernels for 2%

profile of v4, /device:TPU:1, one launch (start us, length us, event | category | flops | bytes accessed | tf_op | source)
XLA Modules:
  0.0 177.7 jit_solution(17049148439115114001)
XLA Ops:
  7.2 0.0 reduce-scatter.2.cloned.1.call-start
  7.2 1.6 shard_map.110
  8.8 33.5 %all_gather.3.held_ref = bf16[64,4224]{1,0:T(8,128)(2,1)S(1)} all-gather(bf16[16,4224]{1,0:T(8,128)(2,1)} %shard_map.110), channel_id=1, replica_groups=mesh['y'=8,'core'=2,'x'=4,'zh'=4,'zl'=4] {'zh'}, dimensions={0}, use_global_device_ids=true | all-gather | bytes 675840 | tf_op jit(solution)/shard_map/all_gather | solution.py:282
  42.4 0.0 copy-start.2
  42.4 1.0 shard_map.111
  43.4 0.0 copy-start
  43.5 0.0 copy-start.1
  43.5 52.7 %all_to_all.25 = bf16[16,16,4096]{2,1,0:T(8,128)(2,1)S(1)} all-to-all(bf16[16,16,4096]{2,1,0:T(8,128)(2,1)S(1)} %bitcast.28), channel_id=1, replica_groups={{0,1,2,3,16,17,18,19,32,33,34,35,48,49,50,51},{4,5,6,7,20,21,22,23,36,3..., dimensions={0} | all-to-all | bytes 4194304 | tf_op jit(solution)/shard_map/all_to_all | solution.py:259
  96.2 0.0 copy-done.2
  96.2 0.0 copy-done
  96.2 0.0 copy-done.1
  96.2 4.8 %shard_map.112 = (bf16[256,384]{1,0:T(8,128)(2,1)S(1)}, bf16[256,384]{1,0:T(8,128)(2,1)S(1)}, bf16[256,384]{1,0:T(8,128)(2,1)S(1)}, bf16[256,128]{1,0:T(8,128)(2,1)S(1)}, bf16[8,3,128,384]{3,2,1,0:T(8,128)(2,1)S(1)}) custom-call(s32[1]{0:T(128)} %bitcast.7.core_ref, bf16[256,4096]{1,0:T(8,128)(2,1)S(1)} %bitcast.20, bf16[2048,384]{1,0:T(8,128)(2,1)S(1)} %bitcast.22, ...), custom_call_target="tpu_custom_call" | custom-call | flops 1811939328 | bytes 10000000 | tf_op jit(solution)/shard_map/pallas_call | solution.py:301
  101.0 1.9 %collective-permute-start = (bf16[8,3,128,384]{3,2,1,0:T(8,128)(2,1)S(1)}, bf16[8,3,128,384]{3,2,1,0:T(8,128)(2,1)S(1)}, u32[]{:S(2)}, u32[]{:S(2)}) collective-permute-start(bf16[8,3,128,384]{3,2,1,0:T(8,128)(2,1)S(1)} %get-tuple-element.48), channel_id=1, source_target_pairs={{0,64},{64,0},{1,65},{65,1},{2,66},{66,2},{3,67},{67,3},{4,68},{68... | collective-permute-start | bytes 7077896 | tf_op jit(solution)/shard_map/ppermute | solution.py:312
  102.9 1.1 shard_map.113.own_ref
  104.0 1.3 shard_map.115
  105.3 2.2 %collective-permute-done.arrived_ref = bf16[8,3,128,384]{3,2,1,0:T(8,128)(2,1)S(1)} collective-permute-done((bf16[8,3,128,384]{3,2,1,0:T(8,128)(2,1)S(1)}, bf16[8,3,128,384]{3,2,1,0:T(8,128)(2,1)S(1)}, u32[]{:S(2)}, u32[]{:S(2)}) %collective-permute-start) | collective-permute-done | bytes 2359328 | tf_op jit(solution)/shard_map/ppermute | solution.py:312
  107.4 1.6 shard_map.114
  109.0 0.0 reduce-scatter.2.cloned.1.call-update
  109.0 1.2 slice.3
  110.9 58.1 %conditional.1 = ((bf16[16,2048]{1,0:T(8,128)(2,1)}, bf16[8,16]{1,0:T(8,128)(2,1)})) conditional(s32[]{:T(128)} %bitcast.6, (bf16[256,2176]{1,0:T(8,128)(2,1)S(1)}, bf16[64,256]{1,0:T(8,128)(2,1)S(1)}, bf16[64,128]{1,0:T(8,128)(2,1)S(1)}, f32[1,256]{1,0:T(1,128)S(1)}) %tuple.16, (bf16[256,2176]{1,0:T(8,128)(2,1)S(1)}, bf16[64,256]{1,0:T(8,128)(2,1)S(1)}, ...), branch_computations={%region_0.1_spmd, %region_1.2_spmd} | conditional | flops 67108864 | bytes 5112968 | solution.py:369
  110.9 29.0 %all_to_all.23 = bf16[16,16,2176]{2,1,0:T(8,128)(2,1)S(1)} all-to-all(bf16[16,16,2176]{2,1,0:T(8,128)(2,1)S(1)} %bitcast.33), channel_id=1, replica_groups={{0,1,2,3,16,17,18,19,32,33,34,35,48,49,50,51},{4,5,6,7,20,21,22,23,36,3..., dimensions={0} | all-to-all | bytes 2228224 | tf_op jit(solution)/shard_map/cond/branch_1_fun/all_to_all | solution.py:259
  139.9 0.6 branch_1_fun.2
  140.5 27.8 %all_to_all.24.parts_ref = bf16[4,16,2176]{2,1,0:T(8,128)(2,1)S(1)} all-to-all(bf16[4,16,2176]{2,1,0:T(8,128)(2,1)S(1)} %bitcast.31), channel_id=1, replica_groups=mesh['y'=8,'core'=2,'x'=4,'zh'=4,'zl'=4] {'zh'}, dimensions={0} | all-to-all | bytes 557056 | tf_op jit(solution)/shard_map/cond/branch_1_fun/all_to_all | solution.py:358
  168.3 0.7 branch_1_fun.3
  169.0 0.0 reduce-scatter.2.cloned.1.call-done.total_ref
  169.0 0.0 copy-start.3
  169.0 1.0 copy-done.3
  170.0 0.9 shard_map.116
  (1 shorter events, 0.0 us)
Async XLA Ops:
  7.2 161.8 %reduce-scatter.2.cloned.1.call-start = ((), (), s32[]{:S(2)}) async-start(), calls=%async_computation.6 | async-start | bytes 2654208 | tf_op jit(solution)/shard_map/reduce_scatter | solution.py:336
  42.4 53.8 %copy-start.2 = (bf16[1,384,2048]{2,1,0:T(8,128)(2,1)S(1)}, bf16[1,384,2048]{2,1,0:T(8,128)(2,1)}, u32[]{:S(2)}) copy-start(bf16[1,384,2048]{2,1,0:T(8,128)(2,1)} %param.15) | copy-start | bytes 4718596
  43.4 52.7 %copy-start = (bf16[1,2048,384]{2,1,0:T(8,128)(2,1)S(1)}, bf16[1,2048,384]{2,1,0:T(8,128)(2,1)}, u32[]{:S(2)}) copy-start(bf16[1,2048,384]{2,1,0:T(8,128)(2,1)} %param.13) | copy-start | bytes 4718596
  43.5 52.7 %copy-start.1 = (bf16[1,2048,384]{2,1,0:T(8,128)(2,1)S(1)}, bf16[1,2048,384]{2,1,0:T(8,128)(2,1)}, u32[]{:S(2)}) copy-start(bf16[1,2048,384]{2,1,0:T(8,128)(2,1)} %param.14) | copy-start | bytes 4718596
  101.0 6.4 %collective-permute-start = (bf16[8,3,128,384]{3,2,1,0:T(8,128)(2,1)S(1)}, bf16[8,3,128,384]{3,2,1,0:T(8,128)(2,1)S(1)}, u32[]{:S(2)}, u32[]{:S(2)}) collective-permute-start(bf16[8,3,128,384]{3,2,1,0:T(8,128)(2,1)S(1)} %get-tuple-element.48), channel_id=1, source_target_pairs={{0,64},{64,0},{1,65},{65,1},{2,66},{66,2},{3,67},{67,3},{4,68},{68... | collective-permute-start | bytes 7077896 | tf_op jit(solution)/shard_map/ppermute | solution.py:312
  169.0 1.0 copy-start.3
Sparse Core Ops, SparseCore 0:
  109.1 41.2 reduce-scatter.1

commit v5 on v3

--- a/solution.py
+++ b/solution.py
@@ -109,8 +109,6 @@
     up_back_ref,
     route_ref,
     other_ref,
-    buffer,
-    sems,
 ):
     width = came_ref.shape[1] // 2
     inputs, scaled = came_ref[:, :width], came_ref[:, width:]
@@ -131,13 +129,8 @@
     route_ref[...] = jnp.where(
         lane == 0, high, jnp.where(lane == 1, route - high, 0.0)
     ).astype(BF)
-    copies = []
     for y in range(nblock // 2):
-        weight_terms(nblock, y, 1 - core_ref[0], came_ref, hidden, gate_back, up_back, buffer)
-        copies.append(pltpu.make_async_copy(buffer.at[y], other_ref.at[y], sems.at[y]))
-        copies[-1].start()
-    for copy in copies:
-        copy.wait()
+        weight_terms(nblock, y, 1 - core_ref[0], came_ref, hidden, gate_back, up_back, other_ref)
 
 
 def weight_terms(nblock, y, core, came_ref, hidden, gate_back, up_back, out_ref):
@@ -312,8 +305,6 @@
         9 * slots * ff * width,
         10_000_000,
         ins=[smem] + [VMEM] * 4,
-        out_specs=(VMEM,) * 4 + (APART,),
-        scratch=[pltpu.VMEM(shape, BF), pltpu.SemaphoreType.DMA((ny,))],
         limit=28,
         exps=slots * ff,
     )(core_at, came, gate_w, up_w, down_w)
@@ -331,6 +322,7 @@
         5_000_000,
         ins=[smem] + [VMEM] * 4,
     )(core_at, came, hidden, gate_back, up_back)
+    own, back = lax.optimization_barrier((own, back))
     pair = call(
         add_body,
         terms,
@@ -345,7 +337,6 @@
             pltpu.SemaphoreType.DMA((ny,)),
         ],
     )(own, arrived)
-    pair, back = lax.optimization_barrier((pair, back))
     total = lax.psum_scatter(
         pair.reshape(ny * 3 * block, ff), "y", scatter_dimension=0, tiled=True
     )
@@ -358,6 +349,7 @@
         ),
         0,
         9 * block * ff,
+        limit=60,
     )(total)
 
     back = forward(back)

time: 176 us -> 171 us (0.972); the launches traced: 173 us -> 170 us
  blocking collectives: 86.2 us -> 114 us
  waiting for transfers between devices: 40.5 us -> 16.8 us
  starting transfers between devices: 14.9 us -> 8.82 us
    all_to_all x0 -> x1, blocking collectives: none -> 27.5 us  [shards(): lax.all_to_all(outgoing.reshape(nh, tok, -1), 'zh', split_axis=0, concat_...]
    reduce_scatter x1, waiting for transfers between devices: 19.9 us -> 0.01 us  [shards(): lax.psum_scatter(pair.reshape(ny * 3 * block, ff), 'y', scatter_dimension...]
    all_to_all x1 -> x0, starting transfers between devices: 6.16 us -> none  [shards(): lax.all_to_all(outgoing.reshape(nh, tok, -1), 'zh', split_axis=0, concat_...]
    all_to_all x1, waiting for transfers between devices: 18.8 us -> 16.8 us  [forward(): lax.all_to_all(a.reshape(dests, per, -1), ('core', 'x', 'zh', 'zl'), spli...]
  transfers between devices with their start and end apart: 4 -> 3, of which waited for: 3 -> 1; matrix products, arithmetic and copies ran while one was open for 0% -> 0% of each run, Pallas kernels for 3% -> 4%
where the time goes in v5:
time: 171 us; the launch traced here: 170 us
  blocking collectives  114 us (67%)
  waiting for transfers between devices  16.8 us (10%)
  Pallas kernels  15 us (9%)
  between operations  14.2 us (8%)
  starting transfers between devices  8.82 us (5%)
    all_to_all x1, blocking collectives, forward(): lax.all_to_all(a.reshape(dests, per, -1), ('core', 'x', 'zh', 'zl'), spli...  52.7 us
    all_gather x1, blocking collectives, shards(): gathered = lax.all_gather(packed, 'zh', axis=0, tiled=True)  33.5 us
    all_to_all x1, blocking collectives, shards(): lax.all_to_all(outgoing.reshape(nh, tok, -1), 'zh', split_axis=0, concat_...  27.5 us
    all_to_all x1, waiting for transfers between devices, forward(): lax.all_to_all(a.reshape(dests, per, -1), ('core', 'x', 'zh', 'zl'), spli...  16.8 us
    all_to_all x1, starting transfers between devices, forward(): lax.all_to_all(a.reshape(dests, per, -1), ('core', 'x', 'zh', 'zl'), spli...  6.88 us
    pallas_call x1, Pallas kernels, shards(): call(functools.partial(expert_body, nblock), (small, small, small, jax.Sh...  4.22 us
  transfers between devices with their start and end apart: 3, of which 1 were waited for; matrix products, arithmetic and copies ran while one was open for 0% of the time, Pallas kernels for 4%

profile of v5, /device:TPU:1, one launch (start us, length us, event | category | flops | bytes accessed | tf_op | source)
XLA Modules:
  0.0 169.6 jit_solution(13647117384427677958)
XLA Ops:
  7.2 1.6 shard_map.110
  8.8 33.5 %all_gather.3.held_ref = bf16[64,4224]{1,0:T(8,128)(2,1)S(1)} all-gather(bf16[16,4224]{1,0:T(8,128)(2,1)} %shard_map.110), channel_id=1, replica_groups=mesh['y'=8,'core'=2,'x'=4,'zh'=4,'zl'=4] {'zh'}, dimensions={0}, use_global_device_ids=true | all-gather | bytes 675840 | tf_op jit(solution)/shard_map/all_gather | solution.py:283
  42.3 0.0 copy-start.3
  42.4 1.0 shard_map.111
  43.4 0.0 copy-start
  43.4 0.0 copy-start.1
  43.4 52.7 %all_to_all.15 = bf16[16,16,4096]{2,1,0:T(8,128)(2,1)S(1)} all-to-all(bf16[16,16,4096]{2,1,0:T(8,128)(2,1)S(1)} %bitcast.24), channel_id=1, replica_groups={{0,1,2,3,16,17,18,19,32,33,34,35,48,49,50,51},{4,5,6,7,20,21,22,23,36,3..., dimensions={0} | all-to-all | bytes 4194304 | tf_op jit(solution)/shard_map/all_to_all | solution.py:260
  96.1 0.0 copy-done.3
  96.1 0.0 copy-done
  96.1 0.0 copy-done.1
  96.1 4.2 %shard_map.112 = (bf16[256,384]{1,0:T(8,128)(2,1)S(1)}, bf16[256,384]{1,0:T(8,128)(2,1)S(1)}, bf16[256,384]{1,0:T(8,128)(2,1)S(1)}, bf16[256,128]{1,0:T(8,128)(2,1)S(1)}, bf16[8,3,128,384]{3,2,1,0:T(8,128)(2,1)}) custom-call(s32[1]{0:T(128)} %bitcast.core_ref, bf16[256,4096]{1,0:T(8,128)(2,1)S(1)} %bitcast.16, bf16[2048,384]{1,0:T(8,128)(2,1)S(1)} %bitcast.18, ...), custom_call_target="tpu_custom_call" | custom-call | flops 1811939328 | bytes 10000000 | tf_op jit(solution)/shard_map/pallas_call | solution.py:302
  100.4 1.9 %collective-permute-start = (bf16[8,3,128,384]{3,2,1,0:T(8,128)(2,1)}, bf16[8,3,128,384]{3,2,1,0:T(8,128)(2,1)}, u32[]{:S(2)}, u32[]{:S(2)}) collective-permute-start(bf16[8,3,128,384]{3,2,1,0:T(8,128)(2,1)} %get-tuple-element.31), channel_id=1, source_target_pairs={{0,64},{64,0},{1,65},{65,1},{2,66},{66,2},{3,67},{67,3},{4,68},{68... | collective-permute-start | bytes 7077896 | tf_op jit(solution)/shard_map/ppermute | solution.py:311
  102.3 1.1 shard_map.113.own_ref
  103.3 1.3 shard_map.114
  104.6 0.0 copy-start.2
  104.7 1.0 copy-done.2
  105.7 6.9 %all-to-all-start.1 = ((bf16[16,16,2176]{2,1,0:T(8,128)(2,1)}), bf16[16,16,2176]{2,1,0:T(8,128)(2,1)S(1)}, u32[]{:S(2)}, u32[]{:S(2)}) async-start(bf16[16,16,2176]{2,1,0:T(8,128)(2,1)} %bitcast.23), calls=%async_computation.1 | async-start | bytes 2228224 | tf_op jit(solution)/shard_map/all_to_all | solution.py:260
  112.6 0.0 reduce-scatter.2.cloned.1.call-start
  112.6 0.0 collective-permute-done.arrived_ref
  112.6 2.6 %shard_map.117 = bf16[8,3,128,384]{3,2,1,0:T(8,128)(2,1)} custom-call(bf16[8,3,128,384]{3,2,1,0:T(8,128)(2,1)S(1)} %shard_map.113.own_ref, bf16[8,3,128,384]{3,2,1,0:T(8,128)(2,1)} %collective-permute-done.arrived_ref), custom_call_target="tpu_custom_call" | custom-call | bytes 7000000 | tf_op jit(solution)/shard_map/pallas_call | solution.py:326
  115.2 0.0 reduce-scatter.2.cloned.1.call-update
  115.2 16.8 %all-to-all-done.1 = bf16[16,16,2176]{2,1,0:T(8,128)(2,1)S(1)} async-done(((bf16[16,16,2176]{2,1,0:T(8,128)(2,1)}), bf16[16,16,2176]{2,1,0:T(8,128)(2,1)S(1)}, u32[]{:S(2)}, u32[]{:S(2)}) %all-to-all-start.1) | async-done | bytes 1114144 | tf_op jit(solution)/shard_map/all_to_all | solution.py:260
  132.0 0.6 shard_map.115
  132.7 27.5 %all_to_all.16.parts_ref = bf16[4,16,2176]{2,1,0:T(8,128)(2,1)S(1)} all-to-all(bf16[4,16,2176]{2,1,0:T(8,128)(2,1)S(1)} %bitcast.26), channel_id=1, replica_groups=mesh['y'=8,'core'=2,'x'=4,'zh'=4,'zl'=4] {'zh'}, dimensions={0} | all-to-all | bytes 557056 | tf_op jit(solution)/shard_map/all_to_all | solution.py:362
  160.2 0.7 shard_map.116
  160.9 0.0 reduce-scatter.2.cloned.1.call-done.total_ref
  160.9 1.8 %shard_map.118 = (f32[128,384]{1,0:T(8,128)}, f32[128,384]{1,0:T(8,128)}, f32[384,128]{1,0:T(8,128)}) custom-call(bf16[384,384]{1,0:T(8,128)(2,1)} %reduce-scatter.2.cloned.1.call-done.total_ref), custom_call_target="tpu_custom_call" | custom-call | bytes 442368 | tf_op jit(solution)/shard_map/pallas_call | solution.py:343
  (1 shorter events, 0.0 us)
Async XLA Ops:
  42.3 53.8 %copy-start.3 = (bf16[1,384,2048]{2,1,0:T(8,128)(2,1)S(1)}, bf16[1,384,2048]{2,1,0:T(8,128)(2,1)}, u32[]{:S(2)}) copy-start(bf16[1,384,2048]{2,1,0:T(8,128)(2,1)} %param.13) | copy-start | bytes 4718596
  43.4 52.7 %copy-start = (bf16[1,2048,384]{2,1,0:T(8,128)(2,1)S(1)}, bf16[1,2048,384]{2,1,0:T(8,128)(2,1)}, u32[]{:S(2)}) copy-start(bf16[1,2048,384]{2,1,0:T(8,128)(2,1)} %param.11) | copy-start | bytes 4718596
  43.4 52.7 %copy-start.1 = (bf16[1,2048,384]{2,1,0:T(8,128)(2,1)S(1)}, bf16[1,2048,384]{2,1,0:T(8,128)(2,1)}, u32[]{:S(2)}) copy-start(bf16[1,2048,384]{2,1,0:T(8,128)(2,1)} %param.12) | copy-start | bytes 4718596
  100.4 12.2 %collective-permute-start = (bf16[8,3,128,384]{3,2,1,0:T(8,128)(2,1)}, bf16[8,3,128,384]{3,2,1,0:T(8,128)(2,1)}, u32[]{:S(2)}, u32[]{:S(2)}) collective-permute-start(bf16[8,3,128,384]{3,2,1,0:T(8,128)(2,1)} %get-tuple-element.31), channel_id=1, source_target_pairs={{0,64},{64,0},{1,65},{65,1},{2,66},{66,2},{3,67},{67,3},{4,68},{68... | collective-permute-start | bytes 7077896 | tf_op jit(solution)/shard_map/ppermute | solution.py:311
  104.6 1.0 copy-start.2
  105.7 26.4 %all-to-all-start.1 = ((bf16[16,16,2176]{2,1,0:T(8,128)(2,1)}), bf16[16,16,2176]{2,1,0:T(8,128)(2,1)S(1)}, u32[]{:S(2)}, u32[]{:S(2)}) async-start(bf16[16,16,2176]{2,1,0:T(8,128)(2,1)} %bitcast.23), calls=%async_computation.1 | async-start | bytes 2228224 | tf_op jit(solution)/shard_map/all_to_all | solution.py:260
  112.6 48.3 %reduce-scatter.2.cloned.1.call-start = ((), (), s32[]{:S(2)}) async-start(), calls=%async_computation.4 | async-start | bytes 2654208 | tf_op jit(solution)/shard_map/reduce_scatter | solution.py:340
Sparse Core Ops, SparseCore 0:
  116.8 42.5 reduce-scatter.1

commit v6 on v5

--- a/solution.py
+++ b/solution.py
@@ -31,7 +31,7 @@
     )
 
 
-def pack_body(top, tokens_ref, cots_ref, ids_ref, weights_ref, out_ref, ids_here, weights_here, sems):
+def pack_body(top, tokens_ref, cots_ref, ids_ref, weights_ref, out_ref, ids_here, weights_here, meta_here, sems):
     width = tokens_ref.shape[1]
     copies = [
         pltpu.make_async_copy(source, target, sems.at[n])
@@ -61,9 +61,14 @@
         FIRST,
         preferred_element_type=F32,
     )
-    out_ref[:, 2 * width :] = meta.astype(BF)
+    meta_here[...] = meta.astype(BF)
+    last = pltpu.make_async_copy(
+        meta_here, out_ref.at[:, pl.ds(2 * width, META)], sems.at[4]
+    )
+    last.start()
     copies[2].wait()
     copies[3].wait()
+    last.wait()
 
 
 def select_body(tok, cap, top, held_ref, dest_ref, send_ref, pick_ref, meta_ref):
@@ -109,28 +114,44 @@
     up_back_ref,
     route_ref,
     other_ref,
+    gate_here,
+    up_here,
+    back_here,
 ):
-    width = came_ref.shape[1] // 2
+    slots, width = came_ref.shape[0], came_ref.shape[1] // 2
     inputs, scaled = came_ref[:, :width], came_ref[:, width:]
-    pre_gate = jnp.dot(inputs, gate_ref[...], preferred_element_type=F32)
-    pre_up = jnp.dot(inputs, up_ref[...], preferred_element_type=F32)
-    back_hidden = lax.dot_general(scaled, down_ref[...], LAST, preferred_element_type=F32)
-    sigma = 1.0 / (1.0 + jnp.exp(-pre_gate))
-    active = pre_gate * sigma
-    hidden = (active * pre_up).astype(BF)
-    gate_back = (back_hidden * pre_up * sigma * (1.0 + pre_gate * (1.0 - sigma))).astype(BF)
-    up_back = (back_hidden * active).astype(BF)
-    hidden_ref[...] = hidden
-    gate_back_ref[...] = gate_back
-    up_back_ref[...] = up_back
-    route = jnp.sum(hidden.astype(F32) * back_hidden, axis=1, keepdims=True)
-    high = route.astype(BF).astype(F32)
-    lane = lax.broadcasted_iota(jnp.int32, route_ref.shape, 1)
-    route_ref[...] = jnp.where(
-        lane == 0, high, jnp.where(lane == 1, route - high, 0.0)
-    ).astype(BF)
+    gate_here[...] = jnp.dot(inputs, gate_ref[...], preferred_element_type=F32)
+    up_here[...] = jnp.dot(inputs, up_ref[...], preferred_element_type=F32)
+    back_here[...] = lax.dot_general(scaled, down_ref[...], LAST, preferred_element_type=F32)
+    step = 32
+    for row in range(0, slots, step):
+        rows = pl.ds(row, step)
+        pre_gate, pre_up, back_hidden = gate_here[rows, :], up_here[rows, :], back_here[rows, :]
+        sigma = 1.0 / (1.0 + jnp.exp(-pre_gate))
+        active = pre_gate * sigma
+        hidden = (active * pre_up).astype(BF)
+        hidden_ref[rows, :] = hidden
+        gate_back_ref[rows, :] = (
+            back_hidden * pre_up * sigma * (1.0 + pre_gate * (1.0 - sigma))
+        ).astype(BF)
+        up_back_ref[rows, :] = (back_hidden * active).astype(BF)
+        route = jnp.sum(hidden.astype(F32) * back_hidden, axis=1, keepdims=True)
+        high = route.astype(BF).astype(F32)
+        lane = lax.broadcasted_iota(jnp.int32, (step, META), 1)
+        route_ref[rows, :] = jnp.where(
+            lane == 0, high, jnp.where(lane == 1, route - high, 0.0)
+        ).astype(BF)
     for y in range(nblock // 2):
-        weight_terms(nblock, y, 1 - core_ref[0], came_ref, hidden, gate_back, up_back, other_ref)
+        weight_terms(
+            nblock,
+            y,
+            1 - core_ref[0],
+            came_ref,
+            hidden_ref[...],
+            gate_back_ref[...],
+            up_back_ref[...],
+            other_ref,
+        )
 
 
 def weight_terms(nblock, y, core, came_ref, hidden, gate_back, up_back, out_ref):
@@ -169,7 +190,7 @@
         read.start()
     for y in range(steps):
         reads[y].wait()
-        went[y] = (own_ref[y].astype(F32) + came[y].astype(F32)).astype(BF)
+        went[y] = own_ref[y] + came[y]
         writes[y].start()
     for write in writes:
         write.wait()
@@ -272,11 +293,12 @@
         0,
         4 * tok * width,
         ins=[APART] * 4,
-        out_specs=VMEM,
+        out_specs=APART,
         scratch=[
             pltpu.VMEM((top, tok), jnp.int32),
             pltpu.VMEM((top, tok), BF),
-            pltpu.SemaphoreType.DMA((4,)),
+            pltpu.VMEM((tok, META), BF),
+            pltpu.SemaphoreType.DMA((5,)),
         ],
         limit=60,
     )(tokens, out_grad, expert_ids.T, route_weights.T)
@@ -305,6 +327,7 @@
         9 * slots * ff * width,
         10_000_000,
         ins=[smem] + [VMEM] * 4,
+        scratch=[pltpu.VMEM((slots, ff), F32)] * 3,
         limit=28,
         exps=slots * ff,
     )(core_at, came, gate_w, up_w, down_w)

time: 171 us -> 175 us (1.023)
  Pallas kernels: 15 us -> 18.5 us
    pallas_call x1, Pallas kernels: 1.6 us -> 5.12 us  [shards(): call(functools.partial(pack_body, top), jax.ShapeDtypeStruct((tok, 2 * wi...]
where the time goes in v6:
time: 175 us; the launch traced here: 173 us
  blocking collectives  114 us (65%)
  Pallas kernels  18.5 us (11%)
  waiting for transfers between devices  16.9 us (10%)
  between operations  14.2 us (8%)
  starting transfers between devices  8.83 us (5%)
    all_to_all x1, blocking collectives, forward(): lax.all_to_all(a.reshape(dests, per, -1), ('core', 'x', 'zh', 'zl'), spli...  52.7 us
    all_gather x1, blocking collectives, shards(): gathered = lax.all_gather(packed, 'zh', axis=0, tiled=True)  33.5 us
    all_to_all x1, blocking collectives, shards(): lax.all_to_all(outgoing.reshape(nh, tok, -1), 'zh', split_axis=0, concat_...  27.5 us
    all_to_all x1, waiting for transfers between devices, forward(): lax.all_to_all(a.reshape(dests, per, -1), ('core', 'x', 'zh', 'zl'), spli...  16.9 us
    all_to_all x1, starting transfers between devices, forward(): lax.all_to_all(a.reshape(dests, per, -1), ('core', 'x', 'zh', 'zl'), spli...  6.89 us
    pallas_call x1, Pallas kernels, shards(): call(functools.partial(pack_body, top), jax.ShapeDtypeStruct((tok, 2 * wi...  5.12 us
    pallas_call x1, Pallas kernels, shards(): call(functools.partial(expert_body, nblock), (small, small, small, jax.Sh...  4.31 us
  transfers between devices with their start and end apart: 3, of which 1 were waited for; matrix products, arithmetic and copies ran while one was open for 0% of the time, Pallas kernels for 4%

profile of v6, /device:TPU:1, one launch (start us, length us, event | category | flops | bytes accessed | tf_op | source)
XLA Modules:
  0.0 173.2 jit_solution(15495830034193284429)
XLA Ops:
  7.2 5.1 %shard_map.110 = bf16[16,4224]{1,0:T(8,128)(2,1)} custom-call(bf16[16,2048]{1,0:T(8,128)(2,1)} %tokens_ref.1, bf16[16,2048]{1,0:T(8,128)(2,1)} %cots_ref.1, s32[8,16]{1,0:T(8,128)} %bitcast.27, bf16[8,16]{1,0:T(8,128)(2,1)} %bitcast.28), custom_call_target="tpu_custom_call" | custom-call | bytes 131072 | tf_op jit(solution)/shard_map/pallas_call | solution.py:290
  12.4 33.5 %all_gather.3.held_ref = bf16[64,4224]{1,0:T(8,128)(2,1)S(1)} all-gather(bf16[16,4224]{1,0:T(8,128)(2,1)} %shard_map.110), channel_id=1, replica_groups=mesh['y'=8,'core'=2,'x'=4,'zh'=4,'zl'=4] {'zh'}, dimensions={0}, use_global_device_ids=true | all-gather | bytes 675840 | tf_op jit(solution)/shard_map/all_gather | solution.py:305
  45.9 0.0 copy-start.3
  45.9 1.0 shard_map.111
  46.9 0.0 copy-start
  46.9 0.0 copy-start.1
  46.9 52.7 %all_to_all.15 = bf16[16,16,4096]{2,1,0:T(8,128)(2,1)S(1)} all-to-all(bf16[16,16,4096]{2,1,0:T(8,128)(2,1)S(1)} %bitcast.24), channel_id=1, replica_groups={{0,1,2,3,16,17,18,19,32,33,34,35,48,49,50,51},{4,5,6,7,20,21,22,23,36,3..., dimensions={0} | all-to-all | bytes 4194304 | tf_op jit(solution)/shard_map/all_to_all | solution.py:281
  99.6 0.0 copy-done.3
  99.6 0.0 copy-done
  99.6 0.0 copy-done.1
  99.7 4.3 %shard_map.112 = (bf16[256,384]{1,0:T(8,128)(2,1)S(1)}, bf16[256,384]{1,0:T(8,128)(2,1)S(1)}, bf16[256,384]{1,0:T(8,128)(2,1)S(1)}, bf16[256,128]{1,0:T(8,128)(2,1)S(1)}, bf16[8,3,128,384]{3,2,1,0:T(8,128)(2,1)}) custom-call(s32[1]{0:T(128)} %bitcast.core_ref, bf16[256,4096]{1,0:T(8,128)(2,1)S(1)} %bitcast.16, bf16[2048,384]{1,0:T(8,128)(2,1)S(1)} %bitcast.18, ...), custom_call_target="tpu_custom_call" | custom-call | flops 1811939328 | bytes 10000000 | tf_op jit(solution)/shard_map/pallas_call | solution.py:324
  104.0 1.9 %collective-permute-start = (bf16[8,3,128,384]{3,2,1,0:T(8,128)(2,1)}, bf16[8,3,128,384]{3,2,1,0:T(8,128)(2,1)}, u32[]{:S(2)}, u32[]{:S(2)}) collective-permute-start(bf16[8,3,128,384]{3,2,1,0:T(8,128)(2,1)} %get-tuple-element.31), channel_id=1, source_target_pairs={{0,64},{64,0},{1,65},{65,1},{2,66},{66,2},{3,67},{67,3},{4,68},{68... | collective-permute-start | bytes 7077896 | tf_op jit(solution)/shard_map/ppermute | solution.py:334
  105.9 1.1 shard_map.113.own_ref
  106.9 1.3 shard_map.114
  108.2 0.0 copy-start.2
  108.3 1.0 copy-done.2
  109.3 6.9 %all-to-all-start.1 = ((bf16[16,16,2176]{2,1,0:T(8,128)(2,1)}), bf16[16,16,2176]{2,1,0:T(8,128)(2,1)S(1)}, u32[]{:S(2)}, u32[]{:S(2)}) async-start(bf16[16,16,2176]{2,1,0:T(8,128)(2,1)} %bitcast.23), calls=%async_computation.1 | async-start | bytes 2228224 | tf_op jit(solution)/shard_map/all_to_all | solution.py:281
  116.2 0.0 reduce-scatter.2.cloned.1.call-start
  116.2 0.0 collective-permute-done.arrived_ref
  116.2 2.5 %shard_map.117 = bf16[8,3,128,384]{3,2,1,0:T(8,128)(2,1)} custom-call(bf16[8,3,128,384]{3,2,1,0:T(8,128)(2,1)S(1)} %shard_map.113.own_ref, bf16[8,3,128,384]{3,2,1,0:T(8,128)(2,1)} %collective-permute-done.arrived_ref), custom_call_target="tpu_custom_call" | custom-call | bytes 7000000 | tf_op jit(solution)/shard_map/pallas_call | solution.py:349
  118.8 0.0 reduce-scatter.2.cloned.1.call-update
  118.8 16.9 %all-to-all-done.1 = bf16[16,16,2176]{2,1,0:T(8,128)(2,1)S(1)} async-done(((bf16[16,16,2176]{2,1,0:T(8,128)(2,1)}), bf16[16,16,2176]{2,1,0:T(8,128)(2,1)S(1)}, u32[]{:S(2)}, u32[]{:S(2)}) %all-to-all-start.1) | async-done | bytes 1114144 | tf_op jit(solution)/shard_map/all_to_all | solution.py:281
  135.7 0.6 shard_map.115
  136.3 27.5 %all_to_all.16.parts_ref = bf16[4,16,2176]{2,1,0:T(8,128)(2,1)S(1)} all-to-all(bf16[4,16,2176]{2,1,0:T(8,128)(2,1)S(1)} %bitcast.26), channel_id=1, replica_groups=mesh['y'=8,'core'=2,'x'=4,'zh'=4,'zl'=4] {'zh'}, dimensions={0} | all-to-all | bytes 557056 | tf_op jit(solution)/shard_map/all_to_all | solution.py:385
  163.8 0.7 shard_map.116
  164.5 0.0 reduce-scatter.2.cloned.1.call-done.total_ref
  164.5 1.8 %shard_map.118 = (f32[128,384]{1,0:T(8,128)}, f32[128,384]{1,0:T(8,128)}, f32[384,128]{1,0:T(8,128)}) custom-call(bf16[384,384]{1,0:T(8,128)(2,1)} %reduce-scatter.2.cloned.1.call-done.total_ref), custom_call_target="tpu_custom_call" | custom-call | bytes 442368 | tf_op jit(solution)/shard_map/pallas_call | solution.py:366
  (1 shorter events, 0.0 us)
Async XLA Ops:
  45.9 53.8 %copy-start.3 = (bf16[1,384,2048]{2,1,0:T(8,128)(2,1)S(1)}, bf16[1,384,2048]{2,1,0:T(8,128)(2,1)}, u32[]{:S(2)}) copy-start(bf16[1,384,2048]{2,1,0:T(8,128)(2,1)} %param.13) | copy-start | bytes 4718596
  46.9 52.7 %copy-start = (bf16[1,2048,384]{2,1,0:T(8,128)(2,1)S(1)}, bf16[1,2048,384]{2,1,0:T(8,128)(2,1)}, u32[]{:S(2)}) copy-start(bf16[1,2048,384]{2,1,0:T(8,128)(2,1)} %param.11) | copy-start | bytes 4718596
  46.9 52.7 %copy-start.1 = (bf16[1,2048,384]{2,1,0:T(8,128)(2,1)S(1)}, bf16[1,2048,384]{2,1,0:T(8,128)(2,1)}, u32[]{:S(2)}) copy-start(bf16[1,2048,384]{2,1,0:T(8,128)(2,1)} %param.12) | copy-start | bytes 4718596
  104.0 12.3 %collective-permute-start = (bf16[8,3,128,384]{3,2,1,0:T(8,128)(2,1)}, bf16[8,3,128,384]{3,2,1,0:T(8,128)(2,1)}, u32[]{:S(2)}, u32[]{:S(2)}) collective-permute-start(bf16[8,3,128,384]{3,2,1,0:T(8,128)(2,1)} %get-tuple-element.31), channel_id=1, source_target_pairs={{0,64},{64,0},{1,65},{65,1},{2,66},{66,2},{3,67},{67,3},{4,68},{68... | collective-permute-start | bytes 7077896 | tf_op jit(solution)/shard_map/ppermute | solution.py:334
  108.2 1.0 copy-start.2
  109.3 26.4 %all-to-all-start.1 = ((bf16[16,16,2176]{2,1,0:T(8,128)(2,1)}), bf16[16,16,2176]{2,1,0:T(8,128)(2,1)S(1)}, u32[]{:S(2)}, u32[]{:S(2)}) async-start(bf16[16,16,2176]{2,1,0:T(8,128)(2,1)} %bitcast.23), calls=%async_computation.1 | async-start | bytes 2228224 | tf_op jit(solution)/shard_map/all_to_all | solution.py:281
  116.2 48.3 %reduce-scatter.2.cloned.1.call-start = ((), (), s32[]{:S(2)}) async-start(), calls=%async_computation.4 | async-start | bytes 2654208 | tf_op jit(solution)/shard_map/reduce_scatter | solution.py:363
Sparse Core Ops, SparseCore 0:
  120.4 42.5 reduce-scatter.1

commit v7 on v5

--- a/solution.py
+++ b/solution.py
@@ -248,10 +248,12 @@
         for c in range(nc)
         for b in range(nh)
     ]
+    groups = [g if n < nh else g[::-1] for n, g in enumerate(groups)]
     core = lax.axis_index("core")
     z = lax.axis_index("zh") * nl + lax.axis_index("zl")
     first = (z - core * shift + nz) % nz // nl * nl + core * shift
     dest = jnp.arange(slots, dtype=jnp.int32) // per
+    dest = jnp.where(core == 0, dest, dests - 1 - dest)
     dest_ids = (dest // nl) * nz + (first + dest % nl) % nz
     dest_ids = dest_ids.astype(F32).reshape(1, slots)
     core_at = core.reshape(1).astype(jnp.int32)

time: 171 us -> 172 us (level)
  waiting for transfers between devices: 16.8 us -> 19 us
    all_to_all x1, blocking collectives: 52.7 us -> 55.5 us  [forward(): lax.all_to_all(a.reshape(dests, per, -1), ('core', 'x', 'zh', 'zl'), spli...]
    all_to_all x1, waiting for transfers between devices: 16.8 us -> 19 us  [forward(): lax.all_to_all(a.reshape(dests, per, -1), ('core', 'x', 'zh', 'zl'), spli...]
    all_to_all x1, blocking collectives: 27.5 us -> 25.6 us  [shards(): lax.all_to_all(outgoing.reshape(nh, tok, -1), 'zh', split_axis=0, concat_...]
where the time goes in v7:
time: 172 us; the launch traced here: 171 us
  blocking collectives  115 us (67%)
  waiting for transfers between devices  19 us (11%)
  Pallas kernels  15 us (9%)
  between operations  14.2 us (8%)
  starting transfers between devices  7.25 us (4%)
    all_to_all x1, blocking collectives, forward(): lax.all_to_all(a.reshape(dests, per, -1), ('core', 'x', 'zh', 'zl'), spli...  55.5 us
    all_gather x1, blocking collectives, shards(): gathered = lax.all_gather(packed, 'zh', axis=0, tiled=True)  33.5 us
    all_to_all x1, blocking collectives, shards(): lax.all_to_all(outgoing.reshape(nh, tok, -1), 'zh', split_axis=0, concat_...  25.6 us
    all_to_all x1, waiting for transfers between devices, forward(): lax.all_to_all(a.reshape(dests, per, -1), ('core', 'x', 'zh', 'zl'), spli...  19 us
    all_to_all x1, starting transfers between devices, forward(): lax.all_to_all(a.reshape(dests, per, -1), ('core', 'x', 'zh', 'zl'), spli...  5.3 us
    pallas_call x1, Pallas kernels, shards(): call(functools.partial(expert_body, nblock), (small, small, small, jax.Sh...  4.22 us
  transfers between devices with their start and end apart: 3, of which 1 were waited for; matrix products, arithmetic and copies ran while one was open for 0% of the time, Pallas kernels for 4%

profile of v7, /device:TPU:1, one launch (start us, length us, event | category | flops | bytes accessed | tf_op | source)
XLA Modules:
  0.0 171.1 jit_solution(7488897905907622900)
XLA Ops:
  7.2 1.6 shard_map.110
  8.8 33.5 %all_gather.3.held_ref = bf16[64,4224]{1,0:T(8,128)(2,1)S(1)} all-gather(bf16[16,4224]{1,0:T(8,128)(2,1)} %shard_map.110), channel_id=1, replica_groups=mesh['y'=8,'core'=2,'x'=4,'zh'=4,'zl'=4] {'zh'}, dimensions={0}, use_global_device_ids=true | all-gather | bytes 675840 | tf_op jit(solution)/shard_map/all_gather | solution.py:285
  42.4 0.0 copy-start.3
  42.4 1.0 shard_map.111
  43.4 0.0 copy-start
  43.4 0.0 copy-start.1
  43.4 55.5 %all_to_all.15 = bf16[16,16,4096]{2,1,0:T(8,128)(2,1)S(1)} all-to-all(bf16[16,16,4096]{2,1,0:T(8,128)(2,1)S(1)} %bitcast.24), channel_id=1, replica_groups={{0,1,2,3,16,17,18,19,32,33,34,35,48,49,50,51},{4,5,6,7,20,21,22,23,36,3..., dimensions={0} | all-to-all | bytes 4194304 | tf_op jit(solution)/shard_map/all_to_all | solution.py:262
  99.0 0.0 copy-done.3
  99.0 0.0 copy-done
  99.0 0.0 copy-done.1
  99.0 4.2 %shard_map.112 = (bf16[256,384]{1,0:T(8,128)(2,1)S(1)}, bf16[256,384]{1,0:T(8,128)(2,1)S(1)}, bf16[256,384]{1,0:T(8,128)(2,1)S(1)}, bf16[256,128]{1,0:T(8,128)(2,1)S(1)}, bf16[8,3,128,384]{3,2,1,0:T(8,128)(2,1)}) custom-call(s32[1]{0:T(128)} %bitcast.core_ref, bf16[256,4096]{1,0:T(8,128)(2,1)S(1)} %bitcast.16, bf16[2048,384]{1,0:T(8,128)(2,1)S(1)} %bitcast.18, ...), custom_call_target="tpu_custom_call" | custom-call | flops 1811939328 | bytes 10000000 | tf_op jit(solution)/shard_map/pallas_call | solution.py:304
  103.2 1.9 %collective-permute-start = (bf16[8,3,128,384]{3,2,1,0:T(8,128)(2,1)}, bf16[8,3,128,384]{3,2,1,0:T(8,128)(2,1)}, u32[]{:S(2)}, u32[]{:S(2)}) collective-permute-start(bf16[8,3,128,384]{3,2,1,0:T(8,128)(2,1)} %get-tuple-element.31), channel_id=1, source_target_pairs={{0,64},{64,0},{1,65},{65,1},{2,66},{66,2},{3,67},{67,3},{4,68},{68... | collective-permute-start | bytes 7077896 | tf_op jit(solution)/shard_map/ppermute | solution.py:313
  105.1 1.1 shard_map.113.own_ref
  106.2 1.3 shard_map.114
  107.5 0.0 copy-start.2
  107.5 1.0 copy-done.2
  108.5 5.3 %all-to-all-start.1 = ((bf16[16,16,2176]{2,1,0:T(8,128)(2,1)}), bf16[16,16,2176]{2,1,0:T(8,128)(2,1)S(1)}, u32[]{:S(2)}, u32[]{:S(2)}) async-start(bf16[16,16,2176]{2,1,0:T(8,128)(2,1)} %bitcast.23), calls=%async_computation.1 | async-start | bytes 2228224 | tf_op jit(solution)/shard_map/all_to_all | solution.py:262
  113.8 0.0 reduce-scatter.2.cloned.1.call-start
  113.9 0.0 collective-permute-done.arrived_ref
  113.9 2.6 %shard_map.117 = bf16[8,3,128,384]{3,2,1,0:T(8,128)(2,1)} custom-call(bf16[8,3,128,384]{3,2,1,0:T(8,128)(2,1)S(1)} %shard_map.113.own_ref, bf16[8,3,128,384]{3,2,1,0:T(8,128)(2,1)} %collective-permute-done.arrived_ref), custom_call_target="tpu_custom_call" | custom-call | bytes 7000000 | tf_op jit(solution)/shard_map/pallas_call | solution.py:328
  116.5 0.0 reduce-scatter.2.cloned.1.call-update
  116.5 19.0 %all-to-all-done.1 = bf16[16,16,2176]{2,1,0:T(8,128)(2,1)S(1)} async-done(((bf16[16,16,2176]{2,1,0:T(8,128)(2,1)}), bf16[16,16,2176]{2,1,0:T(8,128)(2,1)S(1)}, u32[]{:S(2)}, u32[]{:S(2)}) %all-to-all-start.1) | async-done | bytes 1114144 | tf_op jit(solution)/shard_map/all_to_all | solution.py:262
  135.5 0.6 shard_map.115
  136.1 25.6 %all_to_all.16.parts_ref = bf16[4,16,2176]{2,1,0:T(8,128)(2,1)S(1)} all-to-all(bf16[4,16,2176]{2,1,0:T(8,128)(2,1)S(1)} %bitcast.26), channel_id=1, replica_groups=mesh['y'=8,'core'=2,'x'=4,'zh'=4,'zl'=4] {'zh'}, dimensions={0} | all-to-all | bytes 557056 | tf_op jit(solution)/shard_map/all_to_all | solution.py:364
  161.7 0.7 shard_map.116
  162.4 0.0 reduce-scatter.2.cloned.1.call-done.total_ref
  162.4 1.8 %shard_map.118 = (f32[128,384]{1,0:T(8,128)}, f32[128,384]{1,0:T(8,128)}, f32[384,128]{1,0:T(8,128)}) custom-call(bf16[384,384]{1,0:T(8,128)(2,1)} %reduce-scatter.2.cloned.1.call-done.total_ref), custom_call_target="tpu_custom_call" | custom-call | bytes 442368 | tf_op jit(solution)/shard_map/pallas_call | solution.py:345
  (1 shorter events, 0.0 us)
Async XLA Ops:
  42.4 56.6 %copy-start.3 = (bf16[1,384,2048]{2,1,0:T(8,128)(2,1)S(1)}, bf16[1,384,2048]{2,1,0:T(8,128)(2,1)}, u32[]{:S(2)}) copy-start(bf16[1,384,2048]{2,1,0:T(8,128)(2,1)} %param.13) | copy-start | bytes 4718596
  43.4 55.6 %copy-start = (bf16[1,2048,384]{2,1,0:T(8,128)(2,1)S(1)}, bf16[1,2048,384]{2,1,0:T(8,128)(2,1)}, u32[]{:S(2)}) copy-start(bf16[1,2048,384]{2,1,0:T(8,128)(2,1)} %param.11) | copy-start | bytes 4718596
  43.4 55.5 %copy-start.1 = (bf16[1,2048,384]{2,1,0:T(8,128)(2,1)S(1)}, bf16[1,2048,384]{2,1,0:T(8,128)(2,1)}, u32[]{:S(2)}) copy-start(bf16[1,2048,384]{2,1,0:T(8,128)(2,1)} %param.12) | copy-start | bytes 4718596
  103.2 10.7 %collective-permute-start = (bf16[8,3,128,384]{3,2,1,0:T(8,128)(2,1)}, bf16[8,3,128,384]{3,2,1,0:T(8,128)(2,1)}, u32[]{:S(2)}, u32[]{:S(2)}) collective-permute-start(bf16[8,3,128,384]{3,2,1,0:T(8,128)(2,1)} %get-tuple-element.31), channel_id=1, source_target_pairs={{0,64},{64,0},{1,65},{65,1},{2,66},{66,2},{3,67},{67,3},{4,68},{68... | collective-permute-start | bytes 7077896 | tf_op jit(solution)/shard_map/ppermute | solution.py:313
  107.5 1.0 copy-start.2
  108.5 26.9 %all-to-all-start.1 = ((bf16[16,16,2176]{2,1,0:T(8,128)(2,1)}), bf16[16,16,2176]{2,1,0:T(8,128)(2,1)S(1)}, u32[]{:S(2)}, u32[]{:S(2)}) async-start(bf16[16,16,2176]{2,1,0:T(8,128)(2,1)} %bitcast.23), calls=%async_computation.1 | async-start | bytes 2228224 | tf_op jit(solution)/shard_map/all_to_all | solution.py:262
  113.8 48.6 %reduce-scatter.2.cloned.1.call-start = ((), (), s32[]{:S(2)}) async-start(), calls=%async_computation.4 | async-start | bytes 2654208 | tf_op jit(solution)/shard_map/reduce_scatter | solution.py:342
Sparse Core Ops, SparseCore 0:
  118.1 41.7 reduce-scatter.1
